TPU v7x, 32 devices: a whole 2x2x4 slice. The times are simulated.
32 devices in a mesh: group: 2 (over y), row: 2 (over core), col: 8 (over z, x).
Axes of the slice: x: 2, y: 2, z: 4, core: 2. Of those that a mesh axis runs over, the one named last changes fastest.
Arguments:
- tokens: bfloat16 [1024, 8192], P(('group', 'col'), 'row'), parts along dimension 0, may hold values from -6 to 6
- cotangent: bfloat16 [1024, 8192], P(('group', 'col'), 'row'), parts along dimension 0, may hold values from -6 to 6
- gate_weight: bfloat16 [8192, 16384], P('row', 'col'), may hold values from -0.09375 to 0.09375
- up_weight: bfloat16 [8192, 16384], P('row', 'col'), may hold values from -0.09375 to 0.09375
- down_weight: bfloat16 [16384, 8192], P('col', 'row'), may hold values from -0.0625 to 0.0625
- gate_mask: int32 [64, 128], P('row', 'col'), may hold values from 0 to 1, as said below
- up_mask: int32 [64, 128], P('row', 'col'), may hold values from 0 to 1, as said below
- down_mask: int32 [128, 64], P('col', 'row'), may hold values from 0 to 1, as said below
Outputs:
- output: bfloat16 [1024, 8192], P(('group', 'col'), 'row'), parts along dimension 0
- input_grad: bfloat16 [1024, 8192], P(('group', 'col'), 'row'), parts along dimension 0
- gate_grad: bfloat16 [16384, 16384], P(('group', 'row'), 'col'), parts along dimension 0
- up_grad: bfloat16 [16384, 16384], P(('group', 'row'), 'col'), parts along dimension 0
- down_grad: bfloat16 [32768, 8192], P(('group', 'col'), 'row'), parts along dimension 0
There are 2 independent parts, one for each index of `group`. A program takes and returns all parts, laid end to end along the dimension named above; an argument that names none is the same for every part. Nothing has to cross between parts.
Inputs may be any that keep to these rules, and one draw needn't show every extreme that they name: `gate_mask`: 1 keeps a 128 x 128 block of the projection, 0 removes it. `up_mask`: 1 keeps a 128 x 128 block of the projection, 0 removes it. `down_mask`: 1 keeps a 128 x 128 block of the projection, 0 removes it.
All inputs are finite; a program needn't handle non-finite values.
Results may differ from a plain program's by a relative error of at most 0.005.
Values may be sent and summed in bfloat16 or wider, within the bound.
A program may use at most 320 MiB of HBM per device.

v0:
```python
import jax
import jax.numpy as jnp
from jax import lax
from jax.sharding import PartitionSpec as P

BLOCK = 128


def spread(block_mask):
    row_blocks, col_blocks = block_mask.shape
    expanded = jnp.broadcast_to(
        block_mask.astype(jnp.bfloat16)[:, None, :, None], (row_blocks, BLOCK, col_blocks, BLOCK)
    )
    return expanded.reshape(row_blocks * BLOCK, col_blocks * BLOCK)


def contract_rows(left, right):
    return lax.dot_general(
        left, right, (((0,), (0,)), ((), ())), preferred_element_type=jnp.float32
    )


def body(tokens, cotangent, gate_weight, up_weight, down_weight, gate_mask, up_mask, down_mask):
    gate_keep = spread(gate_mask)
    up_keep = spread(up_mask)
    down_keep = spread(down_mask)
    both_eff = jnp.concatenate([gate_weight * gate_keep, up_weight * up_keep], axis=1)
    down_eff = down_weight * down_keep
    hidden_cols = gate_weight.shape[1]
    gathered = lax.all_gather(tokens, "col", axis=0, tiled=True)
    partial_sums = lax.psum(jnp.dot(gathered, both_eff, preferred_element_type=jnp.float32), "row")
    gate_pre = partial_sums[:, :hidden_cols]
    up_pre = partial_sums[:, hidden_cols:]
    sigmoid_gate = jax.nn.sigmoid(gate_pre)
    activated = gate_pre * sigmoid_gate
    hidden = (activated * up_pre).astype(jnp.bfloat16)
    row_block = hidden
    output = lax.psum_scatter(
        jnp.dot(row_block, down_eff, preferred_element_type=jnp.float32),
        "col",
        scatter_dimension=0,
        tiled=True,
    ).astype(jnp.bfloat16)
    shard_rows = lax.all_gather(cotangent, "col", axis=0, tiled=True)
    term = lax.dot_general(
        shard_rows, down_eff, (((1,), (1,)), ((), ())), preferred_element_type=jnp.float32
    )
    row_block = hidden
    down_total = contract_rows(row_block, shard_rows)
    hidden_grad = lax.psum(term, "row")
    gate_delta = (
        hidden_grad * up_pre * sigmoid_gate * (1.0 + gate_pre * (1.0 - sigmoid_gate))
    ).astype(jnp.bfloat16)
    up_delta = (hidden_grad * activated).astype(jnp.bfloat16)
    both_delta = jnp.concatenate([gate_delta, up_delta], axis=1)
    row_block = both_delta
    input_grad = lax.psum_scatter(
        lax.dot_general(
            row_block, both_eff, (((1,), (1,)), ((), ())), preferred_element_type=jnp.float32
        ),
        "col",
        scatter_dimension=0,
        tiled=True,
    ).astype(jnp.bfloat16)
    features = lax.all_gather(tokens, "col", axis=0, tiled=True)
    gate_grad = (contract_rows(features, gate_delta) * gate_keep).astype(jnp.bfloat16)
    up_grad = (contract_rows(features, up_delta) * up_keep).astype(jnp.bfloat16)
    down_grad = (down_total * down_keep).astype(jnp.bfloat16)
    return (output, input_grad, gate_grad, up_grad, down_grad)


def solution(mesh):
    in_specs = (
        P(("group", "col"), "row"),
        P(("group", "col"), "row"),
        P("row", "col"),
        P("row", "col"),
        P("col", "row"),
        P("row", "col"),
        P("row", "col"),
        P("col", "row"),
    )
    out_specs = (
        P(("group", "col"), "row"),
        P(("group", "col"), "row"),
        P(("group", "row"), "col"),
        P(("group", "row"), "col"),
        P(("group", "col"), "row"),
    )
    return jax.shard_map(body, mesh=mesh, in_specs=in_specs, out_specs=out_specs, check_vma=False)
```

profile of v0, /device:TPU:0, one launch (start us, length us, event | category | flops | bytes accessed | tf_op | source)
XLA Modules:
  0.0 578.7 jit_solution(12022222742906459888)
XLA Ops:
  7.2 0.0 all-gather.5.cloned.1.call-start
  7.2 0.7 all-gather.5.cloned.1.call-update
  7.9 0.0 all-gather.3.cloned.1.call-start
  7.9 0.7 all-gather.3.cloned.1.call-update
  8.6 0.0 all-reduce.3.cloned.1.call-start
  8.7 0.7 convert_element_type.42
  9.4 0.7 convert_element_type.43
  10.1 0.7 convert_element_type.45
  10.8 21.2 %copy.13 = bf16[4096,2048]{0,1:T(8,128)(2,1)} copy(bf16[4096,2048]{1,0:T(8,128)(2,1)} %param.10) | data formatting | bytes 33554432 | tf_op args[2]
  32.0 21.4 %copy.14 = bf16[4096,2048]{0,1:T(8,128)(2,1)} copy(bf16[4096,2048]{1,0:T(8,128)(2,1)} %param.11) | data formatting | bytes 33554432 | tf_op args[3]
  53.5 6.2 %broadcast_in_dim.7 = bf16[32,128,16,128]{1,0,3,2:T(8,128)(2,1)} broadcast(bf16[32,16]{0,1:T(8,128)(2,1)S(1)} %convert_element_type.43), dimensions={0,2} | broadcast | bytes 16778240 | tf_op jit(solution)/shard_map/broadcast_in_dim | solution.py:11
  59.7 2.8 broadcast_in_dim.6
  62.5 0.0 copy-start
  62.5 5.7 copy-done
  68.2 30.1 %bitcast_multiply_fusion.3 = (bf16[4096,2048]{0,1:T(8,128)(2,1)}, bf16[4096,2048]{0,1:T(8,128)(2,1)}) fusion(bf16[4096,2048]{0,1:T(8,128)(2,1)} %copy.14, bf16[256,8,32,128]{3,2,1,0:T(8,128)(2,1)} %bitcast.46, bf16[4096,2048]{0,1:T(8,128)(2,1)} %copy.13, bf16[256,8,32,128]{3,2,1,0:T(8,128)(2,1)S(1)} %bitcast.44), kind=kLoop, calls=%fused_computation.9 | loop fusion | flops 16777216 | bytes 100663296 | tf_op jit(solution)/shard_map/mul | solution.py:27
  98.3 0.0 all-gather.5.cloned.1.call-done
  98.3 6.3 %broadcast_in_dim.8 = bf16[16,128,32,128]{3,2,1,0:T(8,128)(2,1)} broadcast(bf16[16,32]{1,0:T(8,128)(2,1)S(1)} %convert_element_type.45), dimensions={0,2} | broadcast | bytes 16778240 | tf_op jit(solution)/shard_map/broadcast_in_dim | solution.py:11
  104.6 19.3 %fusion.11 = f32[512,2048]{0,1:T(8,128)} fusion(bf16[512,4096]{1,0:T(8,128)(2,1)} %all-gather.5.cloned.1.call-done, bf16[2048,4096]{1,0:T(8,128)(2,1)} %param.12, bf16[256,8,32,128]{3,2,1,0:T(8,128)(2,1)} %bitcast.48), kind=kOutput, calls=%fused_computation.22 | convolution fusion | flops 8598323200 | bytes 41943040 | tf_op jit(solution)/shard_map/dot_general | solution.py:45
  123.9 36.2 %all-gather.3.cloned.1.call-done = bf16[512,4096]{1,0:T(8,128)(2,1)} async-done(((bf16[64,4096]{1,0:T(8,128)(2,1)}), bf16[512,4096]{1,0:T(8,128)(2,1)}) %all-gather.3.cloned.1.call-update) | async-done | bytes 4194320 | tf_op jit(solution)/shard_map/all_gather | solution.py:30
  160.1 24.5 %fusion.4 = f32[512,4096]{0,1:T(8,128)} fusion(bf16[512,4096]{1,0:T(8,128)(2,1)} %all-gather.3.cloned.1.call-done, bf16[4096,2048]{0,1:T(8,128)(2,1)} %get-tuple-element.15, bf16[4096,2048]{0,1:T(8,128)(2,1)} %get-tuple-element.16), kind=kOutput, calls=%fused_computation.11 | convolution fusion | flops 17246978048 | bytes 46137344 | tf_op jit(solution)/shard_map/dot_general | solution.py:31
  184.6 0.0 all-reduce.3.cloned.1.call-update
  184.6 0.0 reduce-scatter.5.cloned.1.call-start
  184.7 47.9 %all-reduce.3.cloned.1.call-done = (f32[512,4096]{0,1:T(8,128)}, f32[512,2048]{0,1:T(8,128)}) async-done(((f32[512,4096]{0,1:T(8,128)}, f32[512,2048]{0,1:T(8,128)}), (f32[512,4096]{0,1:T(8,128)}, f32[512,2048]{0,1:T(8,128)})) %all-reduce.3.cloned.1.call-update) | async-done | bytes 12582928 | tf_op jit(solution)/shard_map/psum | solution.py:31
  232.6 7.4 %multiply_convert_fusion.2 = (bf16[512,2048]{0,1:T(8,128)(2,1)}, bf16[512,2048]{0,1:T(8,128)(2,1)}, bf16[512,2048]{0,1:T(8,128)(2,1)S(1)}) fusion(f32[512,2048]{0,1:T(8,128)} %get-tuple-element.11, f32[512,4096]{0,1:T(8,128)} %get-tuple-element.10), kind=kLoop, calls=%fused_computation.18 | loop fusion | flops 15728640 | bytes 18874368 | tf_op jit(solution)/shard_map/convert_element_type | solution.py:53
  240.0 27.4 %fusion.2 = f32[512,4096]{1,0:T(8,128)} fusion(bf16[4096,2048]{0,1:T(8,128)(2,1)} %get-tuple-element.15, bf16[4096,2048]{0,1:T(8,128)(2,1)} %get-tuple-element.16, bf16[512,2048]{0,1:T(8,128)(2,1)} %get-tuple-element.13, bf16[512,2048]{0,1:T(8,128)(2,1)} %get-tuple-element.12), kind=kOutput, calls=%fused_computation.6 | convolution fusion | flops 17255366656 | bytes 46137344 | tf_op jit(solution)/shard_map/dot_general | solution.py:58
  267.4 0.0 reduce-scatter.5.cloned.1.call-update
  267.4 0.0 reduce-scatter.3.cloned.1.call-start
  267.5 18.2 %fusion.6 = f32[512,4096]{1,0:T(8,128)} fusion(bf16[512,2048]{0,1:T(8,128)(2,1)S(1)} %get-tuple-element.14, bf16[2048,4096]{1,0:T(8,128)(2,1)} %param.12, bf16[256,8,32,128]{3,2,1,0:T(8,128)(2,1)} %bitcast.49), kind=kOutput, calls=%fused_computation.13 | convolution fusion | flops 8598323200 | bytes 44040192 | tf_op jit(solution)/shard_map/dot_general | solution.py:39
  285.7 0.0 reduce-scatter.3.cloned.1.call-update
  285.7 19.2 %fusion = bf16[4096,2048]{0,1:T(8,128)(2,1)} fusion(bf16[512,2048]{0,1:T(8,128)(2,1)} %get-tuple-element.13, bf16[512,4096]{1,0:T(8,128)(2,1)} %all-gather.3.cloned.1.call-done, bf16[256,8,32,128]{3,2,1,0:T(8,128)(2,1)} %bitcast.47), kind=kOutput, calls=%fused_computation.2 | convolution fusion | flops 8615100416 | bytes 39845888 | tf_op jit(solution)/shard_map/dot_general | solution.py:18
  304.9 22.5 %copy.16 = bf16[4096,2048]{1,0:T(8,128)(2,1)} copy(bf16[4096,2048]{0,1:T(8,128)(2,1)} %fusion) | data formatting | bytes 33554432
  327.5 19.5 %fusion.1 = bf16[4096,2048]{0,1:T(8,128)(2,1)} fusion(bf16[512,2048]{0,1:T(8,128)(2,1)} %get-tuple-element.12, bf16[512,4096]{1,0:T(8,128)(2,1)} %all-gather.3.cloned.1.call-done, bf16[256,8,32,128]{3,2,1,0:T(8,128)(2,1)} %bitcast.45), kind=kOutput, calls=%fused_computation.4 | convolution fusion | flops 8615100416 | bytes 39845888 | tf_op jit(solution)/shard_map/dot_general | solution.py:18
  347.0 22.5 %copy.15 = bf16[4096,2048]{1,0:T(8,128)(2,1)} copy(bf16[4096,2048]{0,1:T(8,128)(2,1)} %fusion.1) | data formatting | bytes 33554432
  369.4 18.6 %multiply_convert_fusion = bf16[2048,4096]{1,0:T(8,128)(2,1)} fusion(bf16[512,2048]{0,1:T(8,128)(2,1)S(1)} %get-tuple-element.14, bf16[512,4096]{1,0:T(8,128)(2,1)} %all-gather.5.cloned.1.call-done, bf16[256,8,32,128]{3,2,1,0:T(8,128)(2,1)} %bitcast.50), kind=kOutput, calls=%fused_computation.5 | convolution fusion | flops 8615100416 | bytes 39845888 | tf_op jit(solution)/shard_map/dot_general | solution.py:18
  388.1 29.6 %reduce-scatter.5.cloned.1.call-done = f32[64,4096]{1,0:T(8,128)} async-done(((f32[512,4096]{1,0:T(8,128)}), f32[64,4096]{1,0:T(8,128)}) %reduce-scatter.5.cloned.1.call-update) | async-done | bytes 1048592 | tf_op jit(solution)/shard_map/reduce_scatter | solution.py:57
  417.7 2.1 convert_element_type.49
  419.8 149.9 %reduce-scatter.3.cloned.1.call-done = f32[64,4096]{1,0:T(8,128)} async-done(((f32[512,4096]{1,0:T(8,128)}), f32[64,4096]{1,0:T(8,128)}) %reduce-scatter.3.cloned.1.call-update) | async-done | bytes 1048592 | tf_op jit(solution)/shard_map/reduce_scatter | solution.py:38
  569.6 2.1 convert_element_type.46
Async XLA Ops:
  7.2 91.2 %all-gather.5.cloned.1.call-start = ((), (), s32[]{:S(2)}) async-start(), calls=%async_computation.4 | async-start | bytes 4718592 | tf_op jit(solution)/shard_map/all_gather | solution.py:44
  7.9 152.2 %all-gather.3.cloned.1.call-start = ((), (), s32[]{:S(2)}) async-start(), calls=%async_computation.2 | async-start | bytes 4718592 | tf_op jit(solution)/shard_map/all_gather | solution.py:30
  8.6 223.9 %all-reduce.3.cloned.1.call-start = ((), (), s32[]{:S(2)}) async-start(), calls=%async_computation.6 | async-start | bytes 25165824 | tf_op jit(solution)/shard_map/psum | solution.py:31
  62.5 5.7 copy-start
  184.6 233.1 %reduce-scatter.5.cloned.1.call-start = ((), (), s32[]{:S(2)}) async-start(), calls=%async_computation.5 | async-start | bytes 9437184 | tf_op jit(solution)/shard_map/reduce_scatter | solution.py:57
  267.4 302.2 %reduce-scatter.3.cloned.1.call-start = ((), (), s32[]{:S(2)}) async-start(), calls=%async_computation.3 | async-start | bytes 9437184 | tf_op jit(solution)/shard_map/reduce_scatter | solution.py:38
Sparse Core Ops, SparseCore 0:
  10.1 76.0 all-gather.4
  88.4 71.6 all-gather.2
  184.7 47.7 all-reduce.2
  267.5 150.1 reduce-scatter.4
  421.6 147.9 reduce-scatter.2
where the time goes:
time: 588 us; the launch traced here: 579 us
  waiting for transfers between devices  265 us (45%)
  matrix products  147 us (25%)
  local copies, waits for them, and re-layouts  109 us (19%)
  other arithmetic  43.8 us (7%)
  between operations  14.2 us (2%)
    reduce_scatter x1, waiting for transfers between devices, body(): lax.psum_scatter(jnp.dot(row_block, down_eff, preferred_element_type=jnp....  150 us
    unnamed x6, local copies, waits for them, and re-layouts  93.4 us
    dot_general x3, matrix products, contract_rows(): lax.dot_general(left, right, (((0,), (0,)), ((), ())), preferred_element_...  57.4 us
    psum x1, waiting for transfers between devices, body(): lax.psum(jnp.dot(gathered, both_eff, preferred_element_type=jnp.float32),...  47.9 us
    all_gather x1, waiting for transfers between devices, body(): gathered = lax.all_gather(tokens, 'col', axis=0, tiled=True)  36.2 us
    mul x1, other arithmetic, body(): up_weight * up_keep  30.1 us
    reduce_scatter x1, waiting for transfers between devices, body(): lax.psum_scatter(lax.dot_general(row_block, both_eff, (((1,), (1,)), ((),...  29.6 us
    dot_general x1, matrix products, body(): lax.dot_general(row_block, both_eff, (((1,), (1,)), ((), ())), preferred_...  27.4 us
  transfers between devices with their start and end apart: 5, of which 4 were waited for; matrix products, arithmetic and copies ran while one was open for 40% of the time, Pallas kernels for 0%

commit v1 on v0

v1 whole, which is shorter than its diff:
```python
import functools

import jax
import jax.numpy as jnp
from jax import lax
from jax.experimental import pallas as pl
from jax.experimental.pallas import tpu as pltpu
from jax.sharding import PartitionSpec as P

BLOCK = 128
TILE = 256
VMEM_LIMIT = 52 * 1024 * 1024
F32, BF16 = jnp.float32, jnp.bfloat16

WALK = (0, 2, 4, 6, 7, 5, 3, 1)
FORWARD = [(WALK[i], WALK[(i + 1) % 8]) for i in range(8)]
BACKWARD = [(b, a) for a, b in FORWARD]


def dot(left, right, dims):
    return lax.dot_general(left, right, (dims, ((), ())), preferred_element_type=F32)


def keep_rows(flag):
    return jnp.full((1, BLOCK), flag, jnp.int32).astype(F32)


def masked_into(dst, weight, mask, row0, col0):
    for r in range(weight.shape[0] // BLOCK):
        for c in range(weight.shape[1] // BLOCK):
            rows, cols = pl.ds(r * BLOCK, BLOCK), pl.ds(c * BLOCK, BLOCK)
            keep = keep_rows(mask[row0 + r, col0 + c]).astype(BF16)
            dst[rows, cols] = weight[rows, cols] * keep


def call(kernel, grid, ins, in_specs, outs, out_specs, scratch, flops):
    moved = sum(a.size * a.dtype.itemsize for a in [*ins, *outs])
    return pl.pallas_call(
        kernel,
        grid=(grid,),
        in_specs=in_specs,
        out_specs=out_specs,
        out_shape=outs,
        scratch_shapes=scratch,
        compiler_params=pltpu.CompilerParams(vmem_limit_bytes=VMEM_LIMIT),
        cost_estimate=pl.CostEstimate(flops=flops, bytes_accessed=moved, transcendentals=0),
    )(*ins)


def whole(shape):
    return pl.BlockSpec(shape, lambda i: (0, 0))


def by_cols(rows, width):
    return pl.BlockSpec((rows, width), lambda i: (0, i))


def by_rows(height, cols):
    return pl.BlockSpec((height, cols), lambda i: (i, 0))


SMEM = pl.BlockSpec(memory_space=pltpu.SMEM)


def pre_kernel(t, gw, uw, gm, um, g32, u32, g16, u16, ge, ue):
    col0 = pl.program_id(0) * (TILE // BLOCK)
    for w, m, eff, full, short in ((gw, gm, ge, g32, g16), (uw, um, ue, u32, u16)):
        masked_into(eff, w, m, 0, col0)
        total = dot(t[...], eff[...], ((1,), (0,)))
        full[...] = total
        short[...] = total.astype(BF16)


def pre_activations(t, gw, uw, gm, um):
    m, k = t.shape
    n = gw.shape[1]
    outs = [jax.ShapeDtypeStruct((m, n), d) for d in (F32, F32, BF16, BF16)]
    return call(
        pre_kernel, n // TILE, [t, gw, uw, gm, um],
        [whole((m, k)), by_cols(k, TILE), by_cols(k, TILE), SMEM, SMEM],
        outs, [by_cols(m, TILE)] * 4, [pltpu.VMEM((k, TILE), BF16)] * 2, 4 * m * k * n,
    )


def hgrad_kernel(c, dw, dm, full, short, eff):
    masked_into(eff, dw, dm, pl.program_id(0) * (TILE // BLOCK), 0)
    total = dot(c[...], eff[...], ((1,), (1,)))
    full[...] = total
    short[...] = total.astype(BF16)


def hidden_gradient(c, dw, dm):
    m, k = c.shape
    n = dw.shape[0]
    outs = [jax.ShapeDtypeStruct((m, n), d) for d in (F32, BF16)]
    return call(
        hgrad_kernel, n // TILE, [c, dw, dm], [whole((m, k)), by_rows(TILE, k), SMEM],
        outs, [by_cols(m, TILE)] * 2, [pltpu.VMEM((TILE, k), BF16)], 2 * m * k * n,
    )


def out_kernel(h, dw, dm, out, eff):
    masked_into(eff, dw, dm, 0, pl.program_id(0) * (eff.shape[1] // BLOCK))
    out[...] = dot(h[...], eff[...], ((1,), (0,))).astype(out.dtype)


def output_partial(h, dw, dm, dtype):
    m, k = h.shape
    n = dw.shape[1]
    tile = 2 * TILE
    return call(
        out_kernel, n // tile, [h, dw, dm], [whole((m, k)), by_cols(k, tile), SMEM],
        [jax.ShapeDtypeStruct((m, n), dtype)], [by_cols(m, tile)],
        [pltpu.VMEM((k, tile), BF16)], 2 * m * k * n,
    )[0]


def in_kernel(gd, ud, gw, uw, gm, um, out, ge, ue):
    row0 = pl.program_id(0) * (ge.shape[0] // BLOCK)
    masked_into(ge, gw, gm, row0, 0)
    masked_into(ue, uw, um, row0, 0)
    dims = ((1,), (1,))
    out[...] = (dot(gd[...], ge[...], dims) + dot(ud[...], ue[...], dims)).astype(out.dtype)


def input_partial(gd, ud, gw, uw, gm, um, dtype):
    m, k = gd.shape
    n = gw.shape[0]
    tile = 2 * TILE
    return call(
        in_kernel, n // tile, [gd, ud, gw, uw, gm, um],
        [whole((m, k))] * 2 + [by_rows(tile, k)] * 2 + [SMEM] * 2,
        [jax.ShapeDtypeStruct((m, n), dtype)], [by_cols(m, tile)],
        [pltpu.VMEM((tile, k), BF16)] * 2, 4 * m * k * n,
    )[0]


def grads_kernel(count, *refs):
    left = refs[0]
    rights, masks, outs = refs[1:1 + count], refs[1 + count:1 + 2 * count], refs[1 + 2 * count:]
    flipped = left[...].T
    row0 = pl.program_id(0) * (left.shape[1] // BLOCK)
    for right, mask, out in zip(rights, masks, outs):
        for col in range(0, right.shape[1], TILE):
            total = dot(flipped, right[:, col:col + TILE], ((1,), (0,)))
            for r in range(left.shape[1] // BLOCK):
                for c in range(TILE // BLOCK):
                    keep = keep_rows(mask[row0 + r, col // BLOCK + c])
                    part = total[r * BLOCK:(r + 1) * BLOCK, c * BLOCK:(c + 1) * BLOCK]
                    out[pl.ds(r * BLOCK, BLOCK), pl.ds(col + c * BLOCK, BLOCK)] = (part * keep).astype(BF16)


def weight_grads(left, rights, masks):
    m, k = left.shape
    n = rights[0].shape[1]
    tile = min(2 * TILE, k)
    count = len(rights)
    return call(
        functools.partial(grads_kernel, count), k // tile, [left, *rights, *masks],
        [by_cols(m, tile)] + [whole((m, n))] * count + [SMEM] * count,
        [jax.ShapeDtypeStruct((k, n), BF16)] * count, [by_rows(tile, n)] * count, [], 2 * m * k * n * count,
    )


def ring_gather(x):
    half = x.shape[0] // 2
    ahead, behind = [x], [x]
    for _ in range(3):
        behind.append(lax.ppermute(behind[-1], "col", FORWARD))
        ahead.append(lax.ppermute(ahead[-1], "col", BACKWARD))
    top = lax.ppermute(behind[-1][:half], "col", FORWARD)
    bottom = lax.ppermute(ahead[-1][half:], "col", BACKWARD)
    return jnp.concatenate([*ahead, top, bottom, *behind[:0:-1]], axis=0)


def add(a, b):
    return (a.astype(F32) + b.astype(F32)).astype(BF16)


def ring_scatter(partial):
    rows = partial.shape[0] // 8
    half = partial.shape[1] // 2
    part = [partial[j * rows:(j + 1) * rows] for j in range(8)]
    first = lax.ppermute(part[4][:, :half], "col", FORWARD)
    second = lax.ppermute(part[4][:, half:], "col", BACKWARD)
    forward = jnp.concatenate([add(part[3][:, :half], first), part[3][:, half:]], axis=1)
    backward = jnp.concatenate([part[5][:, :half], add(part[5][:, half:], second)], axis=1)
    for step in range(2):
        forward = add(part[2 - step], lax.ppermute(forward, "col", FORWARD))
        backward = add(part[6 + step], lax.ppermute(backward, "col", BACKWARD))
    forward = lax.ppermute(forward, "col", FORWARD)
    backward = lax.ppermute(backward, "col", BACKWARD)
    return (part[0].astype(F32) + forward.astype(F32) + backward.astype(F32)).astype(BF16)


def plain_gather(x):
    return lax.all_gather(x, "col", axis=0, tiled=True)


def plain_scatter(partial):
    return lax.psum_scatter(partial, "col", scatter_dimension=0, tiled=True).astype(BF16)


def body(ring, tokens, cotangent, gate_weight, up_weight, down_weight, gate_mask, up_mask, down_mask):
    gather, scatter = (ring_gather, ring_scatter) if ring else (plain_gather, plain_scatter)
    sent = BF16 if ring else F32

    def other_row(x):
        return lax.ppermute(x, "row", [(0, 1), (1, 0)]).astype(F32)

    features = gather(tokens)
    features, cotangent = lax.optimization_barrier((features, cotangent))
    shard_rows = gather(cotangent)
    gate_own, up_own, gate_sent, up_sent = pre_activations(features, gate_weight, up_weight, gate_mask, up_mask)
    gate_pre = gate_own + other_row(gate_sent)
    up_pre = up_own + other_row(up_sent)
    sigmoid_gate = jax.nn.sigmoid(gate_pre)
    activated = gate_pre * sigmoid_gate
    hidden = (activated * up_pre).astype(BF16)
    output = scatter(output_partial(hidden, down_weight, down_mask, sent))
    grad_own, grad_sent = hidden_gradient(shard_rows, down_weight, down_mask)
    hidden_grad = grad_own + other_row(grad_sent)
    gate_delta = (hidden_grad * up_pre * sigmoid_gate * (1.0 + gate_pre * (1.0 - sigmoid_gate))).astype(BF16)
    up_delta = (hidden_grad * activated).astype(BF16)
    input_grad = scatter(input_partial(gate_delta, up_delta, gate_weight, up_weight, gate_mask, up_mask, sent))
    gate_grad, up_grad = weight_grads(features, [gate_delta, up_delta], [gate_mask, up_mask])
    (down_grad,) = weight_grads(hidden, [shard_rows], [down_mask])
    return (output, input_grad, gate_grad, up_grad, down_grad)


def solution(mesh):
    in_specs = (
        P(("group", "col"), "row"),
        P(("group", "col"), "row"),
        P("row", "col"),
        P("row", "col"),
        P("col", "row"),
        P("row", "col"),
        P("row", "col"),
        P("col", "row"),
    )
    out_specs = (
        P(("group", "col"), "row"),
        P(("group", "col"), "row"),
        P(("group", "row"), "col"),
        P(("group", "row"), "col"),
        P(("group", "col"), "row"),
    )
    step = functools.partial(body, mesh.shape["col"] == 8)
    return jax.shard_map(step, mesh=mesh, in_specs=in_specs, out_specs=out_specs, check_vma=False)
```

time: 588 us -> 331 us (0.56); the launches traced: 579 us -> 330 us
  matrix products: 147 us -> 0 us
  Pallas kernels: 0 us -> 125 us
  waiting for transfers between devices: 265 us -> 144 us
  local copies, waits for them, and re-layouts: 109 us -> 10.3 us
  starting transfers between devices: 0.2 us -> 39.1 us
  other arithmetic: 43.8 us -> 10.2 us
  between operations: 14.2 us -> 0.9 us
    reduce_scatter x2 -> x0, waiting for transfers between devices: 179 us -> none  [the longest x1 150 us: body(): lax.psum_scatter(jnp.dot(row_block, down_eff, preferred_element_type=jnp....]
    dot_general x7 -> x0, matrix products: 147 us -> none  [the longest x3 57.4 us: contract_rows(): lax.dot_general(left, right, (((0,), (0,)), ((), ())), preferred_element_...]
    ppermute x0 -> x35, waiting for transfers between devices: none -> 144 us  [the longest x4 35.7 us: ring_scatter(): forward = add(part[2 - step], lax.ppermute(forward, 'col', FORWARD))]
    pallas_call x0 -> x6, Pallas kernels: none -> 125 us  [call(): pl.pallas_call(kernel, grid=(grid,), in_specs=in_specs, out_specs=out_spe...]
    unnamed x6 -> x36, local copies, waits for them, and re-layouts: 93.4 us -> 9.16 us
    psum x1 -> x0, waiting for transfers between devices: 47.9 us -> none  [body(): lax.psum(jnp.dot(gathered, both_eff, preferred_element_type=jnp.float32),...]
    ppermute x0 -> x35, starting transfers between devices: none -> 39.1 us  [the longest x6 9.71 us: ring_gather(): ahead.append(lax.ppermute(ahead[-1], 'col', BACKWARD))]
    all_gather x2 -> x0, waiting for transfers between devices: 36.2 us -> none  [the longest x1 36.2 us: body(): gathered = lax.all_gather(tokens, 'col', axis=0, tiled=True)]
  transfers between devices with their start and end apart: 5 -> 35, of which waited for: 4 -> 22; matrix products, arithmetic and copies ran while one was open for 40% -> 4% of each run, Pallas kernels for 0% -> 13%
where the time goes in v1:
time: 331 us; the launch traced here: 330 us
  waiting for transfers between devices  144 us (44%)
  Pallas kernels  125 us (38%)
  starting transfers between devices  39.1 us (12%)
  local copies, waits for them, and re-layouts  10.3 us (3%)
  other arithmetic  10.2 us (3%)
    pallas_call x6, Pallas kernels, call(): pl.pallas_call(kernel, grid=(grid,), in_specs=in_specs, out_specs=out_spe...  125 us
    ppermute x4, waiting for transfers between devices, ring_scatter(): forward = add(part[2 - step], lax.ppermute(forward, 'col', FORWARD))  35.7 us
    ppermute x6, waiting for transfers between devices, ring_gather(): ahead.append(lax.ppermute(ahead[-1], 'col', BACKWARD))  29.8 us
    ppermute x6, waiting for transfers between devices, ring_gather(): behind.append(lax.ppermute(behind[-1], 'col', FORWARD))  21.7 us
    ppermute x2, waiting for transfers between devices, ring_scatter(): backward = lax.ppermute(backward, 'col', BACKWARD)  18.5 us
    ppermute x4, waiting for transfers between devices, ring_scatter(): backward = add(part[6 + step], lax.ppermute(backward, 'col', BACKWARD))  12.4 us
    ppermute x6, starting transfers between devices, ring_gather(): ahead.append(lax.ppermute(ahead[-1], 'col', BACKWARD))  9.71 us
    unnamed x36, local copies, waits for them, and re-layouts  9.16 us
  transfers between devices with their start and end apart: 35, of which 22 were waited for; matrix products, arithmetic and copies ran while one was open for 4% of the time, Pallas kernels for 13%

profile of v1, /device:TPU:0, one launch (start us, length us, event | category | flops | bytes accessed | tf_op | source)
XLA Modules:
  0.0 330.0 jit_solution(17536368861486759799)
XLA Ops:
  0.6 3.0 collective-permute-start
  3.8 12.1 %collective-permute-done = bf16[64,4096]{1,0:T(8,128)(2,1)S(1)} collective-permute-done((bf16[64,4096]{1,0:T(8,128)(2,1)}, bf16[64,4096]{1,0:T(8,128)(2,1)S(1)}, u32[]{:S(2)}, u32[]{:S(2)}) %collective-permute-start) | collective-permute-done | bytes 524320 | tf_op jit(solution)/shard_map/ppermute | solution.py:170
  15.8 1.7 collective-permute-start.1
  17.9 1.1 constant_dynamic-update-slice_fusion.8
  19.0 10.0 %collective-permute-done.1 = bf16[64,4096]{1,0:T(8,128)(2,1)S(1)} collective-permute-done((bf16[64,4096]{1,0:T(8,128)(2,1)S(1)}, bf16[64,4096]{1,0:T(8,128)(2,1)S(1)}, u32[]{:S(2)}, u32[]{:S(2)}) %collective-permute-start.1) | collective-permute-done | bytes 524320 | tf_op jit(solution)/shard_map/ppermute | solution.py:170
  29.0 1.3 collective-permute-start.2
  30.3 0.7 collective-permute-start.5
  31.1 11.2 %collective-permute-done.5 = bf16[64,4096]{1,0:T(8,128)(2,1)S(1)} collective-permute-done((bf16[64,4096]{1,0:T(8,128)(2,1)S(1)}, bf16[64,4096]{1,0:T(8,128)(2,1)S(1)}, u32[]{:S(2)}, u32[]{:S(2)}) %collective-permute-start.5) | collective-permute-done | bytes 524320 | tf_op jit(solution)/shard_map/ppermute | solution.py:169
  42.3 0.7 collective-permute-start.6
  43.1 1.4 collective-permute-start.7
  44.5 4.2 %collective-permute-done.6 = bf16[32,4096]{1,0:T(8,128)(2,1)S(1)} collective-permute-done((bf16[32,4096]{1,0:T(8,128)(2,1)S(1)}, bf16[32,4096]{1,0:T(8,128)(2,1)S(1)}, u32[]{:S(2)}, u32[]{:S(2)}) %collective-permute-start.6) | collective-permute-done | bytes 262176 | tf_op jit(solution)/shard_map/ppermute | solution.py:171
  48.8 2.3 collective-permute-done.7
  51.2 1.8 collective-permute-start.18
  53.2 2.1 collective-permute-start.21
  55.5 7.8 %collective-permute-done.18 = bf16[64,4096]{1,0:T(8,128)(2,1)} collective-permute-done((bf16[64,4096]{1,0:T(8,128)(2,1)S(1)}, bf16[64,4096]{1,0:T(8,128)(2,1)}, u32[]{:S(2)}, u32[]{:S(2)}) %collective-permute-start.18) | collective-permute-done | bytes 524320 | tf_op jit(solution)/shard_map/ppermute | solution.py:170
  63.3 1.9 collective-permute-start.19
  65.2 1.5 collective-permute-done.21
  66.7 2.5 collective-permute-start.22
  69.2 26.9 %shard_map.119 = (f32[512,2048]{1,0:T(8,128)}, f32[512,2048]{1,0:T(8,128)}, bf16[512,2048]{1,0:T(8,128)(2,1)}, bf16[512,2048]{1,0:T(8,128)(2,1)}) custom-call(bf16[512,4096]{1,0:T(8,128)(2,1)} %copy-done.6, bf16[4096,2048]{1,0:T(8,128)(2,1)} %gw.3, bf16[4096,2048]{1,0:T(8,128)(2,1)} %uw.3, s32[32,16]{1,0:T(8,128)S(1)} %copy.13.gm.refs_3_, ...), custom_call_target="tpu_custom_call" | custom-call | flops 17179869184 | bytes 50335744 | tf_op jit(solution)/shard_map/pallas_call | solution.py:38
  96.6 0.9 constant_dynamic-update-slice_fusion.17
  97.5 2.3 collective-permute-start.23
  99.8 1.9 constant_dynamic-update-slice_fusion.16
  101.6 0.9 constant_dynamic-update-slice_fusion.15
  102.5 9.0 %collective-permute-done.23 = bf16[64,4096]{1,0:T(8,128)(2,1)S(1)} collective-permute-done((bf16[64,4096]{1,0:T(8,128)(2,1)S(1)}, bf16[64,4096]{1,0:T(8,128)(2,1)S(1)}, u32[]{:S(2)}, u32[]{:S(2)}) %collective-permute-start.23) | collective-permute-done | bytes 524320 | tf_op jit(solution)/shard_map/ppermute | solution.py:169
  111.5 2.3 collective-permute-start.24
  114.0 0.8 constant_dynamic-update-slice_fusion.14
  114.9 4.1 %collective-permute-done.24 = bf16[32,4096]{1,0:T(8,128)(2,1)S(1)} collective-permute-done((bf16[32,4096]{1,0:T(8,128)(2,1)S(1)}, bf16[32,4096]{1,0:T(8,128)(2,1)S(1)}, u32[]{:S(2)}, u32[]{:S(2)}) %collective-permute-start.24) | collective-permute-done | bytes 262176 | tf_op jit(solution)/shard_map/ppermute | solution.py:171
  119.0 0.7 constant_dynamic-update-slice_fusion.13
  119.7 1.5 collective-permute-done.25
  121.2 0.7 constant_dynamic-update-slice_fusion.12
  121.9 0.8 constant_dynamic-update-slice_fusion.11
  122.7 0.8 constant_dynamic-update-slice_fusion.10
  123.5 0.9 constant_dynamic-update-slice_fusion.9.c.refs_1_
  124.4 17.6 %shard_map.121 = (f32[512,2048]{1,0:T(8,128)}, bf16[512,2048]{1,0:T(8,128)(2,1)}) custom-call(bf16[512,4096]{1,0:T(8,128)(2,1)} %constant_dynamic-update-slice_fusion.9.c.refs_1_, bf16[2048,4096]{1,0:T(8,128)(2,1)} %dw.3, s32[16,32]{1,0:T(8,128)S(1)} %copy-done), custom_call_target="tpu_custom_call" | custom-call | flops 8589934592 | bytes 27265024 | tf_op jit(solution)/shard_map/pallas_call | solution.py:38
  142.1 4.4 %collective-permute-done.26 = bf16[512,2048]{1,0:T(8,128)(2,1)S(1)} collective-permute-done((bf16[512,2048]{1,0:T(8,128)(2,1)}, bf16[512,2048]{1,0:T(8,128)(2,1)S(1)}, u32[]{:S(2)}, u32[]{:S(2)}) %collective-permute-start.26) | collective-permute-done | bytes 2097184 | tf_op jit(solution)/shard_map/ppermute | solution.py:209
  146.4 6.8 %multiply_convert_fusion = (bf16[512,2048]{1,0:T(8,128)(2,1)}, bf16[512,2048]{1,0:T(8,128)(2,1)}, bf16[512,2048]{1,0:T(8,128)(2,1)}) fusion(f32[512,2048]{1,0:T(8,128)} %get-tuple-element.21, bf16[512,2048]{1,0:T(8,128)(2,1)S(1)} %collective-permute-done.26, f32[512,2048]{1,0:T(8,128)S(1)} %copy-done.3, bf16[512,2048]{1,0:T(8,128)(2,1)S(1)} %collective-permute-done.8, ...), kind=kLoop, calls=%fused_computation | loop fusion | flops 22020096 | bytes 25165824 | tf_op jit(solution)/shard_map/convert_element_type | solution.py:224
  153.3 26.9 %shard_map.122 = bf16[512,4096]{1,0:T(8,128)(2,1)} custom-call(bf16[512,2048]{1,0:T(8,128)(2,1)} %get-tuple-element.26.gd.refs_1_, bf16[512,2048]{1,0:T(8,128)(2,1)} %get-tuple-element.25.ud.refs_2_, bf16[4096,2048]{1,0:T(8,128)(2,1)} %gw.3, bf16[4096,2048]{1,0:T(8,128)(2,1)} %uw.3, s32[32,16]{1,0:T(8,128)S(1)} %copy.13.gm.refs_3_, s32[32,16]{1,0:T(8,128)S(1)} %copy.14.um.refs_4_), custom_call_target="tpu_custom_call" | custom-call | flops 17179869184 | bytes 41947136 | tf_op jit(solution)/shard_map/pallas_call | solution.py:38
  180.2 23.7 %shard_map.123 = (bf16[4096,2048]{1,0:T(8,128)(2,1)}, bf16[4096,2048]{1,0:T(8,128)(2,1)}) custom-call(bf16[512,4096]{1,0:T(8,128)(2,1)} %copy-done.6, bf16[512,2048]{1,0:T(8,128)(2,1)} %get-tuple-element.26.gd.refs_1_, bf16[512,2048]{1,0:T(8,128)(2,1)} %get-tuple-element.25.ud.refs_2_, s32[32,16]{1,0:T(8,128)S(1)} %copy.13.gm.refs_3_, ...), custom_call_target="tpu_custom_call" | custom-call | flops 17179869184 | bytes 41947136 | tf_op jit(solution)/shard_map/pallas_call | solution.py:38
  204.0 15.9 %shard_map.120 = bf16[512,4096]{1,0:T(8,128)(2,1)} custom-call(bf16[512,2048]{1,0:T(8,128)(2,1)} %get-tuple-element.27.h.refs_0_, bf16[2048,4096]{1,0:T(8,128)(2,1)} %dw.3, s32[16,32]{1,0:T(8,128)S(1)} %copy-done), custom_call_target="tpu_custom_call" | custom-call | flops 8589934592 | bytes 23070720 | tf_op jit(solution)/shard_map/pallas_call | solution.py:38
  219.8 14.2 %shard_map.124 = bf16[2048,4096]{1,0:T(8,128)(2,1)} custom-call(bf16[512,2048]{1,0:T(8,128)(2,1)} %get-tuple-element.27.h.refs_0_, bf16[512,4096]{1,0:T(8,128)(2,1)} %constant_dynamic-update-slice_fusion.9.c.refs_1_, s32[16,32]{1,0:T(8,128)S(1)} %copy-done), custom_call_target="tpu_custom_call" | custom-call | flops 8589934592 | bytes 23070720 | tf_op jit(solution)/shard_map/pallas_call | solution.py:38
  234.1 1.4 collective-permute-start.10
  235.5 0.7 collective-permute-start.14
  236.3 1.4 collective-permute-start.27
  237.7 0.7 collective-permute-start.31
  238.4 4.9 %collective-permute-done.10 = bf16[64,2048]{1,0:T(8,128)(2,1)S(1)} collective-permute-done((bf16[64,2048]{1,0:T(8,128)(2,1)S(1)}, bf16[64,2048]{1,0:T(8,128)(2,1)S(1)}, u32[]{:S(2)}, u32[]{:S(2)}) %collective-permute-start.10) | collective-permute-done | bytes 262176 | tf_op jit(solution)/shard_map/ppermute | solution.py:184
  243.3 1.4 collective-permute-done.14
  244.9 1.6 collective-permute-start.11
  246.5 0.5 collective-permute-start.15
  247.1 1.9 collective-permute-done.27
  248.9 1.4 collective-permute-done.31
  250.5 1.6 collective-permute-start.28
  252.7 7.5 %collective-permute-done.11 = bf16[64,4096]{1,0:T(8,128)(2,1)S(1)} collective-permute-done((bf16[64,4096]{1,0:T(8,128)(2,1)S(1)}, bf16[64,4096]{1,0:T(8,128)(2,1)S(1)}, u32[]{:S(2)}, u32[]{:S(2)}) %collective-permute-start.11) | collective-permute-done | bytes 524320 | tf_op jit(solution)/shard_map/ppermute | solution.py:189
  260.3 1.4 collective-permute-start.12
  261.7 9.7 %collective-permute-done.28 = bf16[64,4096]{1,0:T(8,128)(2,1)S(1)} collective-permute-done((bf16[64,4096]{1,0:T(8,128)(2,1)S(1)}, bf16[64,4096]{1,0:T(8,128)(2,1)S(1)}, u32[]{:S(2)}, u32[]{:S(2)}) %collective-permute-start.28) | collective-permute-done | bytes 524320 | tf_op jit(solution)/shard_map/ppermute | solution.py:189
  271.5 1.4 collective-permute-start.29
  272.9 9.7 %collective-permute-done.12 = bf16[64,4096]{1,0:T(8,128)(2,1)S(1)} collective-permute-done((bf16[64,4096]{1,0:T(8,128)(2,1)S(1)}, bf16[64,4096]{1,0:T(8,128)(2,1)S(1)}, u32[]{:S(2)}, u32[]{:S(2)}) %collective-permute-start.12) | collective-permute-done | bytes 524320 | tf_op jit(solution)/shard_map/ppermute | solution.py:189
  283.2 1.7 collective-permute-start.13
  285.0 8.9 %collective-permute-done.29 = bf16[64,4096]{1,0:T(8,128)(2,1)S(1)} collective-permute-done((bf16[64,4096]{1,0:T(8,128)(2,1)S(1)}, bf16[64,4096]{1,0:T(8,128)(2,1)S(1)}, u32[]{:S(2)}, u32[]{:S(2)}) %collective-permute-start.29) | collective-permute-done | bytes 524320 | tf_op jit(solution)/shard_map/ppermute | solution.py:189
  294.5 1.7 collective-permute-start.30
  296.7 12.4 %collective-permute-done.33 = bf16[64,4096]{1,0:T(8,128)(2,1)S(1)} collective-permute-done((bf16[64,4096]{1,0:T(8,128)(2,1)S(1)}, bf16[64,4096]{1,0:T(8,128)(2,1)S(1)}, u32[]{:S(2)}, u32[]{:S(2)}) %collective-permute-start.33) | collective-permute-done | bytes 524320 | tf_op jit(solution)/shard_map/ppermute | solution.py:190
  309.5 10.8 %collective-permute-done.17 = bf16[64,4096]{1,0:T(8,128)(2,1)S(1)} collective-permute-done((bf16[64,4096]{1,0:T(8,128)(2,1)S(1)}, bf16[64,4096]{1,0:T(8,128)(2,1)S(1)}, u32[]{:S(2)}, u32[]{:S(2)}) %collective-permute-start.17) | collective-permute-done | bytes 524320 | tf_op jit(solution)/shard_map/ppermute | solution.py:192
  320.3 1.0 add_convert_fusion.5
  321.3 7.7 %collective-permute-done.34 = bf16[64,4096]{1,0:T(8,128)(2,1)S(1)} collective-permute-done((bf16[64,4096]{1,0:T(8,128)(2,1)S(1)}, bf16[64,4096]{1,0:T(8,128)(2,1)S(1)}, u32[]{:S(2)}, u32[]{:S(2)}) %collective-permute-start.34) | collective-permute-done | bytes 524320 | tf_op jit(solution)/shard_map/ppermute | solution.py:192
  329.0 1.0 add_convert_fusion
  (71 shorter events, 5.5 us)
Async XLA Ops:
  0.6 15.2 %collective-permute-start = (bf16[64,4096]{1,0:T(8,128)(2,1)}, bf16[64,4096]{1,0:T(8,128)(2,1)S(1)}, u32[]{:S(2)}, u32[]{:S(2)}) collective-permute-start(bf16[64,4096]{1,0:T(8,128)(2,1)} %param.8), channel_id=1, source_target_pairs={{2,0},{4,2},{6,4},{7,6},{5,7},{3,5},{1,3},{0,1},{10,8},{12,10},{14... | collective-permute-start | bytes 1572872 | tf_op jit(solution)/shard_map/ppermute | solution.py:170
  3.6 13.9 %collective-permute-start.3 = (bf16[64,4096]{1,0:T(8,128)(2,1)}, bf16[64,4096]{1,0:T(8,128)(2,1)S(1)}, u32[]{:S(2)}, u32[]{:S(2)}) collective-permute-start(bf16[64,4096]{1,0:T(8,128)(2,1)} %param.8), channel_id=1, source_target_pairs={{0,2},{2,4},{4,6},{6,7},{7,5},{5,3},{3,1},{1,0},{8,10},{10,12},{12... | collective-permute-start | bytes 1572872 | tf_op jit(solution)/shard_map/ppermute | solution.py:169
  15.8 13.1 %collective-permute-start.1 = (bf16[64,4096]{1,0:T(8,128)(2,1)S(1)}, bf16[64,4096]{1,0:T(8,128)(2,1)S(1)}, u32[]{:S(2)}, u32[]{:S(2)}) collective-permute-start(bf16[64,4096]{1,0:T(8,128)(2,1)S(1)} %collective-permute-done), channel_id=1, source_target_pairs={{2,0},{4,2},{6,4},{7,6},{5,7},{3,5},{1,3},{0,1},{10,8},{12,10},{14... | collective-permute-start | bytes 1572872 | tf_op jit(solution)/shard_map/ppermute | solution.py:170
  17.5 12.8 %collective-permute-start.4 = (bf16[64,4096]{1,0:T(8,128)(2,1)S(1)}, bf16[64,4096]{1,0:T(8,128)(2,1)S(1)}, u32[]{:S(2)}, u32[]{:S(2)}) collective-permute-start(bf16[64,4096]{1,0:T(8,128)(2,1)S(1)} %collective-permute-done.3), channel_id=1, source_target_pairs={{0,2},{2,4},{4,6},{6,7},{7,5},{5,3},{3,1},{1,0},{8,10},{10,12},{12... | collective-permute-start | bytes 1572872 | tf_op jit(solution)/shard_map/ppermute | solution.py:169
  18.9 32.2 %copy-start.5 = (bf16[64,4096]{1,0:T(8,128)(2,1)S(1)}, bf16[64,4096]{1,0:T(8,128)(2,1)}, u32[]{:S(2)}) copy-start(bf16[64,4096]{1,0:T(8,128)(2,1)} %param.9) | copy-start | bytes 1572868
  19.0 36.4 %copy-start.7 = (s32[32,16]{0,1:T(8,128)S(1)}, s32[32,16]{0,1:T(8,128)}, u32[]{:S(2)}) copy-start(s32[32,16]{0,1:T(8,128)} %param.13) | copy-start | bytes 6148
  19.0 36.4 %copy-start.8 = (s32[32,16]{0,1:T(8,128)S(1)}, s32[32,16]{0,1:T(8,128)}, u32[]{:S(2)}) copy-start(s32[32,16]{0,1:T(8,128)} %param.14) | copy-start | bytes 6148
  29.0 14.1 %collective-permute-start.2 = (bf16[64,4096]{1,0:T(8,128)(2,1)S(1)}, bf16[64,4096]{1,0:T(8,128)(2,1)S(1)}, u32[]{:S(2)}, u32[]{:S(2)}) collective-permute-start(bf16[64,4096]{1,0:T(8,128)(2,1)S(1)} %collective-permute-done.1), channel_id=1, source_target_pairs={{2,0},{4,2},{6,4},{7,6},{5,7},{3,5},{1,3},{0,1},{10,8},{12,10},{14... | collective-permute-start | bytes 1572872 | tf_op jit(solution)/shard_map/ppermute | solution.py:170
  30.3 12.0 %collective-permute-start.5 = (bf16[64,4096]{1,0:T(8,128)(2,1)S(1)}, bf16[64,4096]{1,0:T(8,128)(2,1)S(1)}, u32[]{:S(2)}, u32[]{:S(2)}) collective-permute-start(bf16[64,4096]{1,0:T(8,128)(2,1)S(1)} %collective-permute-done.4), channel_id=1, source_target_pairs={{0,2},{2,4},{4,6},{6,7},{7,5},{5,3},{3,1},{1,0},{8,10},{10,12},{12... | collective-permute-start | bytes 1572872 | tf_op jit(solution)/shard_map/ppermute | solution.py:169
  42.3 6.4 %collective-permute-start.6 = (bf16[32,4096]{1,0:T(8,128)(2,1)S(1)}, bf16[32,4096]{1,0:T(8,128)(2,1)S(1)}, u32[]{:S(2)}, u32[]{:S(2)}) collective-permute-start(bf16[32,4096]{1,0:T(8,128)(2,1)S(1)} %slice.122), channel_id=1, source_target_pairs={{0,2},{2,4},{4,6},{6,7},{7,5},{5,3},{3,1},{1,0},{8,10},{10,12},{12... | collective-permute-start | bytes 786440 | tf_op jit(solution)/shard_map/ppermute | solution.py:171
  43.1 7.9 %collective-permute-start.7 = (bf16[32,4096]{1,0:T(8,128)(2,1)S(1)}, bf16[32,4096]{1,0:T(8,128)(2,1)S(1)}, u32[]{:S(2)}, u32[]{:S(2)}) collective-permute-start(bf16[32,4096]{1,0:T(8,128)(2,1)S(1)} %slice.123), channel_id=1, source_target_pairs={{2,0},{4,2},{6,4},{7,6},{5,7},{3,5},{1,3},{0,1},{10,8},{12,10},{14... | collective-permute-start | bytes 786440 | tf_op jit(solution)/shard_map/ppermute | solution.py:172
  51.2 2.0 copy-start.6
  51.2 12.1 %collective-permute-start.18 = (bf16[64,4096]{1,0:T(8,128)(2,1)S(1)}, bf16[64,4096]{1,0:T(8,128)(2,1)}, u32[]{:S(2)}, u32[]{:S(2)}) collective-permute-start(bf16[64,4096]{1,0:T(8,128)(2,1)S(1)} %copy-done.5), channel_id=1, source_target_pairs={{2,0},{4,2},{6,4},{7,6},{5,7},{3,5},{1,3},{0,1},{10,8},{12,10},{14... | collective-permute-start | bytes 1572872 | tf_op jit(solution)/shard_map/ppermute | solution.py:170
  53.2 13.6 %collective-permute-start.21 = (bf16[64,4096]{1,0:T(8,128)(2,1)S(1)}, bf16[64,4096]{1,0:T(8,128)(2,1)S(1)}, u32[]{:S(2)}, u32[]{:S(2)}) collective-permute-start(bf16[64,4096]{1,0:T(8,128)(2,1)S(1)} %copy-done.5), channel_id=1, source_target_pairs={{0,2},{2,4},{4,6},{6,7},{7,5},{5,3},{3,1},{1,0},{8,10},{10,12},{12... | collective-permute-start | bytes 1572872 | tf_op jit(solution)/shard_map/ppermute | solution.py:169
  63.3 34.2 %collective-permute-start.19 = (bf16[64,4096]{1,0:T(8,128)(2,1)}, bf16[64,4096]{1,0:T(8,128)(2,1)S(1)}, u32[]{:S(2)}, u32[]{:S(2)}) collective-permute-start(bf16[64,4096]{1,0:T(8,128)(2,1)} %collective-permute-done.18), channel_id=1, source_target_pairs={{2,0},{4,2},{6,4},{7,6},{5,7},{3,5},{1,3},{0,1},{10,8},{12,10},{14... | collective-permute-start | bytes 1572872 | tf_op jit(solution)/shard_map/ppermute | solution.py:170
  66.7 30.8 %collective-permute-start.22 = (bf16[64,4096]{1,0:T(8,128)(2,1)S(1)}, bf16[64,4096]{1,0:T(8,128)(2,1)S(1)}, u32[]{:S(2)}, u32[]{:S(2)}) collective-permute-start(bf16[64,4096]{1,0:T(8,128)(2,1)S(1)} %collective-permute-done.21), channel_id=1, source_target_pairs={{0,2},{2,4},{4,6},{6,7},{7,5},{5,3},{3,1},{1,0},{8,10},{10,12},{12... | collective-permute-start | bytes 1572872 | tf_op jit(solution)/shard_map/ppermute | solution.py:169
  96.1 46.0 %collective-permute-start.8 = (bf16[512,2048]{1,0:T(8,128)(2,1)}, bf16[512,2048]{1,0:T(8,128)(2,1)S(1)}, u32[]{:S(2)}, u32[]{:S(2)}) collective-permute-start(bf16[512,2048]{1,0:T(8,128)(2,1)} %get-tuple-element.17), channel_id=1, source_target_pairs={{0,8},{8,0},{1,9},{9,1},{2,10},{10,2},{3,11},{11,3},{4,12},{12,4},... | collective-permute-start | bytes 6291464 | tf_op jit(solution)/shard_map/ppermute | solution.py:209
  96.1 46.0 %collective-permute-start.9 = (bf16[512,2048]{1,0:T(8,128)(2,1)}, bf16[512,2048]{1,0:T(8,128)(2,1)}, u32[]{:S(2)}, u32[]{:S(2)}) collective-permute-start(bf16[512,2048]{1,0:T(8,128)(2,1)} %get-tuple-element.19), channel_id=1, source_target_pairs={{0,8},{8,0},{1,9},{9,1},{2,10},{10,2},{3,11},{11,3},{4,12},{12,4},... | collective-permute-start | bytes 6291464 | tf_op jit(solution)/shard_map/ppermute | solution.py:209
  97.5 27.0 %copy-start = (s32[16,32]{1,0:T(8,128)S(1)}, s32[16,32]{1,0:T(8,128)}, u32[]{:S(2)}) copy-start(s32[16,32]{1,0:T(8,128)} %refs_2_.1) | copy-start | bytes 6148
  97.5 16.3 %collective-permute-start.20 = (bf16[64,4096]{1,0:T(8,128)(2,1)S(1)}, bf16[64,4096]{1,0:T(8,128)(2,1)S(1)}, u32[]{:S(2)}, u32[]{:S(2)}) collective-permute-start(bf16[64,4096]{1,0:T(8,128)(2,1)S(1)} %collective-permute-done.19), channel_id=1, source_target_pairs={{2,0},{4,2},{6,4},{7,6},{5,7},{3,5},{1,3},{0,1},{10,8},{12,10},{14... | collective-permute-start | bytes 1572872 | tf_op jit(solution)/shard_map/ppermute | solution.py:170
  97.5 14.0 %collective-permute-start.23 = (bf16[64,4096]{1,0:T(8,128)(2,1)S(1)}, bf16[64,4096]{1,0:T(8,128)(2,1)S(1)}, u32[]{:S(2)}, u32[]{:S(2)}) collective-permute-start(bf16[64,4096]{1,0:T(8,128)(2,1)S(1)} %collective-permute-done.22), channel_id=1, source_target_pairs={{0,2},{2,4},{4,6},{6,7},{7,5},{5,3},{3,1},{1,0},{8,10},{10,12},{12... | collective-permute-start | bytes 1572872 | tf_op jit(solution)/shard_map/ppermute | solution.py:169
  111.5 7.5 %collective-permute-start.24 = (bf16[32,4096]{1,0:T(8,128)(2,1)S(1)}, bf16[32,4096]{1,0:T(8,128)(2,1)S(1)}, u32[]{:S(2)}, u32[]{:S(2)}) collective-permute-start(bf16[32,4096]{1,0:T(8,128)(2,1)S(1)} %slice.135), channel_id=1, source_target_pairs={{0,2},{2,4},{4,6},{6,7},{7,5},{5,3},{3,1},{1,0},{8,10},{10,12},{12... | collective-permute-start | bytes 786440 | tf_op jit(solution)/shard_map/ppermute | solution.py:171
  113.8 7.4 %collective-permute-start.25 = (bf16[32,4096]{1,0:T(8,128)(2,1)S(1)}, bf16[32,4096]{1,0:T(8,128)(2,1)S(1)}, u32[]{:S(2)}, u32[]{:S(2)}) collective-permute-start(bf16[32,4096]{1,0:T(8,128)(2,1)S(1)} %slice.136), channel_id=1, source_target_pairs={{2,0},{4,2},{6,4},{7,6},{5,7},{3,5},{1,3},{0,1},{10,8},{12,10},{14... | collective-permute-start | bytes 786440 | tf_op jit(solution)/shard_map/ppermute | solution.py:172
  124.4 22.0 %copy-start.3 = (f32[512,2048]{1,0:T(8,128)S(1)}, f32[512,2048]{1,0:T(8,128)}, u32[]{:S(2)}) copy-start(f32[512,2048]{1,0:T(8,128)} %get-tuple-element.16) | copy-start | bytes 12582916
  124.4 22.0 %copy-start.4 = (f32[512,2048]{1,0:T(8,128)S(1)}, f32[512,2048]{1,0:T(8,128)}, u32[]{:S(2)}) copy-start(f32[512,2048]{1,0:T(8,128)} %get-tuple-element.18) | copy-start | bytes 12582916
  142.1 4.4 %collective-permute-start.26 = (bf16[512,2048]{1,0:T(8,128)(2,1)}, bf16[512,2048]{1,0:T(8,128)(2,1)S(1)}, u32[]{:S(2)}, u32[]{:S(2)}) collective-permute-start(bf16[512,2048]{1,0:T(8,128)(2,1)} %get-tuple-element.22), channel_id=1, source_target_pairs={{0,8},{8,0},{1,9},{9,1},{2,10},{10,2},{3,11},{11,3},{4,12},{12,4},... | collective-permute-start | bytes 6291464 | tf_op jit(solution)/shard_map/ppermute | solution.py:209
  219.8 14.2 %copy-start.2 = (bf16[512,4096]{1,0:T(8,128)(2,1)S(1)}, bf16[512,4096]{1,0:T(8,128)(2,1)}, u32[]{:S(2)}) copy-start(bf16[512,4096]{1,0:T(8,128)(2,1)} %shard_map.120) | copy-start | bytes 12582916
  219.8 16.4 %copy-start.1 = (bf16[512,4096]{1,0:T(8,128)(2,1)S(1)}, bf16[512,4096]{1,0:T(8,128)(2,1)}, u32[]{:S(2)}) copy-start(bf16[512,4096]{1,0:T(8,128)(2,1)} %shard_map.122) | copy-start | bytes 12582916
  234.1 9.2 %collective-permute-start.10 = (bf16[64,2048]{1,0:T(8,128)(2,1)S(1)}, bf16[64,2048]{1,0:T(8,128)(2,1)S(1)}, u32[]{:S(2)}, u32[]{:S(2)}) collective-permute-start(bf16[64,2048]{1,0:T(8,128)(2,1)S(1)} %get-tuple-element.40), channel_id=1, source_target_pairs={{0,2},{2,4},{4,6},{6,7},{7,5},{5,3},{3,1},{1,0},{8,10},{10,12},{12... | collective-permute-start | bytes 786440 | tf_op jit(solution)/shard_map/ppermute | solution.py:184
  235.5 9.2 %collective-permute-start.14 = (bf16[64,2048]{1,0:T(8,128)(2,1)S(1)}, bf16[64,2048]{1,0:T(8,128)(2,1)S(1)}, u32[]{:S(2)}, u32[]{:S(2)}) collective-permute-start(bf16[64,2048]{1,0:T(8,128)(2,1)S(1)} %get-tuple-element.41), channel_id=1, source_target_pairs={{2,0},{4,2},{6,4},{7,6},{5,7},{3,5},{1,3},{0,1},{10,8},{12,10},{14... | collective-permute-start | bytes 786440 | tf_op jit(solution)/shard_map/ppermute | solution.py:185
  236.3 12.6 %collective-permute-start.27 = (bf16[64,2048]{1,0:T(8,128)(2,1)S(1)}, bf16[64,2048]{1,0:T(8,128)(2,1)S(1)}, u32[]{:S(2)}, u32[]{:S(2)}) collective-permute-start(bf16[64,2048]{1,0:T(8,128)(2,1)S(1)} %get-tuple-element.32), channel_id=1, source_target_pairs={{0,2},{2,4},{4,6},{6,7},{7,5},{5,3},{3,1},{1,0},{8,10},{10,12},{12... | collective-permute-start | bytes 786440 | tf_op jit(solution)/shard_map/ppermute | solution.py:184
  237.7 12.6 %collective-permute-start.31 = (bf16[64,2048]{1,0:T(8,128)(2,1)S(1)}, bf16[64,2048]{1,0:T(8,128)(2,1)S(1)}, u32[]{:S(2)}, u32[]{:S(2)}) collective-permute-start(bf16[64,2048]{1,0:T(8,128)(2,1)S(1)} %get-tuple-element.33), channel_id=1, source_target_pairs={{2,0},{4,2},{6,4},{7,6},{5,7},{3,5},{1,3},{0,1},{10,8},{12,10},{14... | collective-permute-start | bytes 786440 | tf_op jit(solution)/shard_map/ppermute | solution.py:185
  244.9 15.3 %collective-permute-start.11 = (bf16[64,4096]{1,0:T(8,128)(2,1)S(1)}, bf16[64,4096]{1,0:T(8,128)(2,1)S(1)}, u32[]{:S(2)}, u32[]{:S(2)}) collective-permute-start(bf16[64,4096]{1,0:T(8,128)(2,1)S(1)} %pad_maximum_fusion), channel_id=1, source_target_pairs={{0,2},{2,4},{4,6},{6,7},{7,5},{5,3},{3,1},{1,0},{8,10},{10,12},{12... | collective-permute-start | bytes 1572872 | tf_op jit(solution)/shard_map/ppermute | solution.py:189
  246.5 26.4 %collective-permute-start.15 = (bf16[64,4096]{1,0:T(8,128)(2,1)S(1)}, bf16[64,4096]{1,0:T(8,128)(2,1)S(1)}, u32[]{:S(2)}, u32[]{:S(2)}) collective-permute-start(bf16[64,4096]{1,0:T(8,128)(2,1)S(1)} %pad_maximum_fusion.1), channel_id=1, source_target_pairs={{2,0},{4,2},{6,4},{7,6},{5,7},{3,5},{1,3},{0,1},{10,8},{12,10},{14... | collective-permute-start | bytes 1572872 | tf_op jit(solution)/shard_map/ppermute | solution.py:190
  250.5 20.9 %collective-permute-start.28 = (bf16[64,4096]{1,0:T(8,128)(2,1)S(1)}, bf16[64,4096]{1,0:T(8,128)(2,1)S(1)}, u32[]{:S(2)}, u32[]{:S(2)}) collective-permute-start(bf16[64,4096]{1,0:T(8,128)(2,1)S(1)} %pad_maximum_fusion.2), channel_id=1, source_target_pairs={{0,2},{2,4},{4,6},{6,7},{7,5},{5,3},{3,1},{1,0},{8,10},{10,12},{12... | collective-permute-start | bytes 1572872 | tf_op jit(solution)/shard_map/ppermute | solution.py:189
  252.2 32.8 %collective-permute-start.32 = (bf16[64,4096]{1,0:T(8,128)(2,1)S(1)}, bf16[64,4096]{1,0:T(8,128)(2,1)S(1)}, u32[]{:S(2)}, u32[]{:S(2)}) collective-permute-start(bf16[64,4096]{1,0:T(8,128)(2,1)S(1)} %pad_maximum_fusion.3), channel_id=1, source_target_pairs={{2,0},{4,2},{6,4},{7,6},{5,7},{3,5},{1,3},{0,1},{10,8},{12,10},{14... | collective-permute-start | bytes 1572872 | tf_op jit(solution)/shard_map/ppermute | solution.py:190
  260.3 22.3 %collective-permute-start.12 = (bf16[64,4096]{1,0:T(8,128)(2,1)S(1)}, bf16[64,4096]{1,0:T(8,128)(2,1)S(1)}, u32[]{:S(2)}, u32[]{:S(2)}) collective-permute-start(bf16[64,4096]{1,0:T(8,128)(2,1)S(1)} %add_convert_fusion.9), channel_id=1, source_target_pairs={{0,2},{2,4},{4,6},{6,7},{7,5},{5,3},{3,1},{1,0},{8,10},{10,12},{12... | collective-permute-start | bytes 1572872 | tf_op jit(solution)/shard_map/ppermute | solution.py:189
  271.5 22.3 %collective-permute-start.29 = (bf16[64,4096]{1,0:T(8,128)(2,1)S(1)}, bf16[64,4096]{1,0:T(8,128)(2,1)S(1)}, u32[]{:S(2)}, u32[]{:S(2)}) collective-permute-start(bf16[64,4096]{1,0:T(8,128)(2,1)S(1)} %add_convert_fusion.4), channel_id=1, source_target_pairs={{0,2},{2,4},{4,6},{6,7},{7,5},{5,3},{3,1},{1,0},{8,10},{10,12},{12... | collective-permute-start | bytes 1572872 | tf_op jit(solution)/shard_map/ppermute | solution.py:189
  282.9 13.3 %collective-permute-start.16 = (bf16[64,4096]{1,0:T(8,128)(2,1)S(1)}, bf16[64,4096]{1,0:T(8,128)(2,1)S(1)}, u32[]{:S(2)}, u32[]{:S(2)}) collective-permute-start(bf16[64,4096]{1,0:T(8,128)(2,1)S(1)} %get-tuple-element.37), channel_id=1, source_target_pairs={{2,0},{4,2},{6,4},{7,6},{5,7},{3,5},{1,3},{0,1},{10,8},{12,10},{14... | collective-permute-start | bytes 1572872 | tf_op jit(solution)/shard_map/ppermute | solution.py:190
  283.2 26.3 %collective-permute-start.13 = (bf16[64,4096]{1,0:T(8,128)(2,1)S(1)}, bf16[64,4096]{1,0:T(8,128)(2,1)S(1)}, u32[]{:S(2)}, u32[]{:S(2)}) collective-permute-start(bf16[64,4096]{1,0:T(8,128)(2,1)S(1)} %get-tuple-element.36), channel_id=1, source_target_pairs={{0,2},{2,4},{4,6},{6,7},{7,5},{5,3},{3,1},{1,0},{8,10},{10,12},{12... | collective-permute-start | bytes 1572872 | tf_op jit(solution)/shard_map/ppermute | solution.py:191
  294.1 14.9 %collective-permute-start.33 = (bf16[64,4096]{1,0:T(8,128)(2,1)S(1)}, bf16[64,4096]{1,0:T(8,128)(2,1)S(1)}, u32[]{:S(2)}, u32[]{:S(2)}) collective-permute-start(bf16[64,4096]{1,0:T(8,128)(2,1)S(1)} %get-tuple-element.29), channel_id=1, source_target_pairs={{2,0},{4,2},{6,4},{7,6},{5,7},{3,5},{1,3},{0,1},{10,8},{12,10},{14... | collective-permute-start | bytes 1572872 | tf_op jit(solution)/shard_map/ppermute | solution.py:190
  294.5 26.8 %collective-permute-start.30 = (bf16[64,4096]{1,0:T(8,128)(2,1)S(1)}, bf16[64,4096]{1,0:T(8,128)(2,1)S(1)}, u32[]{:S(2)}, u32[]{:S(2)}) collective-permute-start(bf16[64,4096]{1,0:T(8,128)(2,1)S(1)} %get-tuple-element.28), channel_id=1, source_target_pairs={{0,2},{2,4},{4,6},{6,7},{7,5},{5,3},{3,1},{1,0},{8,10},{10,12},{12... | collective-permute-start | bytes 1572872 | tf_op jit(solution)/shard_map/ppermute | solution.py:191
  296.3 23.9 %collective-permute-start.17 = (bf16[64,4096]{1,0:T(8,128)(2,1)S(1)}, bf16[64,4096]{1,0:T(8,128)(2,1)S(1)}, u32[]{:S(2)}, u32[]{:S(2)}) collective-permute-start(bf16[64,4096]{1,0:T(8,128)(2,1)S(1)} %add_convert_fusion.6), channel_id=1, source_target_pairs={{2,0},{4,2},{6,4},{7,6},{5,7},{3,5},{1,3},{0,1},{10,8},{12,10},{14... | collective-permute-start | bytes 1572872 | tf_op jit(solution)/shard_map/ppermute | solution.py:192
  309.2 19.8 %collective-permute-start.34 = (bf16[64,4096]{1,0:T(8,128)(2,1)S(1)}, bf16[64,4096]{1,0:T(8,128)(2,1)S(1)}, u32[]{:S(2)}, u32[]{:S(2)}) collective-permute-start(bf16[64,4096]{1,0:T(8,128)(2,1)S(1)} %add_convert_fusion.1), channel_id=1, source_target_pairs={{2,0},{4,2},{6,4},{7,6},{5,7},{3,5},{1,3},{0,1},{10,8},{12,10},{14... | collective-permute-start | bytes 1572872 | tf_op jit(solution)/shard_map/ppermute | solution.py:192

commit v2 on v1

v2 whole, which is shorter than its diff:
```python
import functools

import jax
import jax.numpy as jnp
from jax import lax
from jax.experimental import pallas as pl
from jax.experimental.pallas import tpu as pltpu
from jax.sharding import PartitionSpec as P

BLOCK = 128
TILE = 256
VMEM_LIMIT = 52 * 1024 * 1024
F32, BF16 = jnp.float32, jnp.bfloat16

WALK = (0, 2, 4, 6, 7, 5, 3, 1)
FORWARD = [(WALK[i], WALK[(i + 1) % 8]) for i in range(8)]
BACKWARD = [(b, a) for a, b in FORWARD]


def dot(left, right, dims):
    return lax.dot_general(left, right, (dims, ((), ())), preferred_element_type=F32)


def keep_rows(flag):
    return jnp.full((1, BLOCK), flag, jnp.int32).astype(F32)


def masked_into(dst, weight, mask, row0, col0):
    for r in range(weight.shape[0] // BLOCK):
        for c in range(weight.shape[1] // BLOCK):
            rows, cols = pl.ds(r * BLOCK, BLOCK), pl.ds(c * BLOCK, BLOCK)
            keep = keep_rows(mask[row0 + r, col0 + c]).astype(BF16)
            dst[rows, cols] = weight[rows, cols] * keep


def call(kernel, grid, ins, in_specs, outs, out_specs, scratch, flops, after=(), into=None):
    extra = list(after) + ([] if into is None else [into])
    used, unused = len(ins), len(extra)

    def run(*refs):
        kernel(*refs[:used], *refs[used + unused:])

    moved = sum(a.size * a.dtype.itemsize for a in [*ins, *outs])
    return pl.pallas_call(
        run,
        grid=(grid,),
        in_specs=[*in_specs] + [pl.BlockSpec(memory_space=pl.ANY)] * unused,
        out_specs=out_specs,
        out_shape=outs,
        scratch_shapes=scratch,
        input_output_aliases={} if into is None else {used + unused - 1: 0},
        compiler_params=pltpu.CompilerParams(vmem_limit_bytes=VMEM_LIMIT),
        cost_estimate=pl.CostEstimate(flops=flops, bytes_accessed=moved, transcendentals=0),
    )(*ins, *extra)


def whole(shape):
    return pl.BlockSpec(shape, lambda i: (0, 0))


def by_cols(rows, width, first=0):
    return pl.BlockSpec((rows, width), lambda i: (0, i + first))


def by_rows(height, cols, first=0):
    return pl.BlockSpec((height, cols), lambda i: (i + first, 0))


SMEM = pl.BlockSpec(memory_space=pltpu.SMEM)


def pre_kernel(t, w, m, full, short, eff):
    masked_into(eff, w, m, 0, pl.program_id(0) * (TILE // BLOCK))
    total = dot(t[...], eff[...], ((1,), (0,)))
    full[...] = total
    short[...] = total.astype(BF16)


def pre_activation(t, w, mask, after=()):
    m, k = t.shape
    n = w.shape[1]
    outs = [jax.ShapeDtypeStruct((m, n), d) for d in (F32, BF16)]
    return call(
        pre_kernel, n // TILE, [t, w, mask], [whole((m, k)), by_cols(k, TILE), SMEM],
        outs, [by_cols(m, TILE)] * 2, [pltpu.VMEM((k, TILE), BF16)], 2 * m * k * n, after,
    )


def hgrad_kernel(first, c, dw, dm, out, eff):
    masked_into(eff, dw, dm, (pl.program_id(0) + first) * (TILE // BLOCK), 0)
    out[...] = dot(c[...], eff[...], ((1,), (1,)))


def hidden_gradient(c, dw, dm, first, tiles, after=()):
    m, k = c.shape
    return call(
        functools.partial(hgrad_kernel, first), tiles, [c, dw, dm],
        [whole((m, k)), by_rows(TILE, k, first), SMEM],
        [jax.ShapeDtypeStruct((m, tiles * TILE), F32)], [by_cols(m, TILE)],
        [pltpu.VMEM((TILE, k), BF16)], 2 * m * k * tiles * TILE, after,
    )[0]


def out_kernel(first, h, dw, dm, out, eff):
    masked_into(eff, dw, dm, 0, (pl.program_id(0) + first) * (eff.shape[1] // BLOCK))
    out[...] = dot(h[...], eff[...], ((1,), (0,)))


def output_partial(h, dw, dm, first, tiles, after=()):
    m, k = h.shape
    tile = 2 * TILE
    return call(
        functools.partial(out_kernel, first), tiles, [h, dw, dm],
        [whole((m, k)), by_cols(k, tile, first), SMEM],
        [jax.ShapeDtypeStruct((m, tiles * tile), F32)], [by_cols(m, tile)],
        [pltpu.VMEM((k, tile), BF16)], 2 * m * k * tiles * tile, after,
    )[0]


def in_kernel(first, gd, ud, gw, uw, gm, um, out, ge, ue):
    row0 = (pl.program_id(0) + first) * (ge.shape[0] // BLOCK)
    masked_into(ge, gw, gm, row0, 0)
    masked_into(ue, uw, um, row0, 0)
    dims = ((1,), (1,))
    out[...] = dot(gd[...], ge[...], dims) + dot(ud[...], ue[...], dims)


def input_partial(gd, ud, gw, uw, gm, um, first, tiles, after=()):
    m, k = gd.shape
    tile = 2 * TILE
    return call(
        functools.partial(in_kernel, first), tiles, [gd, ud, gw, uw, gm, um],
        [whole((m, k))] * 2 + [by_rows(tile, k, first)] * 2 + [SMEM] * 2,
        [jax.ShapeDtypeStruct((m, tiles * tile), F32)], [by_cols(m, tile)],
        [pltpu.VMEM((tile, k), BF16)] * 2, 4 * m * k * tiles * tile, after,
    )[0]


def grads_kernel(first, left, right, mask, out):
    flipped = left[...].T
    row0 = (pl.program_id(0) + first) * (left.shape[1] // BLOCK)
    for col in range(0, right.shape[1], TILE):
        total = dot(flipped, right[:, col:col + TILE], ((1,), (0,)))
        for r in range(left.shape[1] // BLOCK):
            for c in range(TILE // BLOCK):
                keep = keep_rows(mask[row0 + r, col // BLOCK + c])
                part = total[r * BLOCK:(r + 1) * BLOCK, c * BLOCK:(c + 1) * BLOCK]
                out[pl.ds(r * BLOCK, BLOCK), pl.ds(col + c * BLOCK, BLOCK)] = (part * keep).astype(BF16)


def weight_grad(left, right, mask, after=(), share=(0, 1), into=None):
    m, k = left.shape
    n = right.shape[1]
    tile = min(2 * TILE, k)
    first = share[0] * (k // tile) // 2 if share[1] == 2 else 0
    last = (share[0] + 1) * (k // tile) // 2 if share[1] == 2 else k // tile
    return call(
        functools.partial(grads_kernel, first), last - first, [left, right, mask],
        [by_cols(m, tile, first), whole((m, n)), SMEM],
        [jax.ShapeDtypeStruct((k, n), BF16)], [by_rows(tile, n, first)], [],
        2 * m * (last - first) * tile * n, after, into,
    )[0]


def ring_gather(x, arrived):
    half = x.shape[0] // 2
    ahead, behind = [x], [x]
    for _ in range(3):
        behind.append(lax.ppermute(behind[-1], "col", FORWARD))
        ahead.append(lax.ppermute(ahead[-1], "col", BACKWARD))
        arrived.append((behind[-1], ahead[-1]))
    top = lax.ppermute(behind[-1][:half], "col", FORWARD)
    bottom = lax.ppermute(ahead[-1][half:], "col", BACKWARD)
    return jnp.concatenate([*ahead, top, bottom, *behind[:0:-1]], axis=0)


def plain_gather(x, arrived):
    arrived.extend([()] * 3)
    return lax.all_gather(x, "col", axis=0, tiled=True)


def ring_scatter(left, right):
    rows = left.shape[0] // 8

    def own(j):
        return left[j * rows:(j + 1) * rows], right[j * rows:(j + 1) * rows]

    sent = own(4)[0].astype(BF16), own(4)[1].astype(BF16)
    yield sent
    first, second = lax.ppermute(sent[0], "col", FORWARD), lax.ppermute(sent[1], "col", BACKWARD)
    forward = jnp.concatenate([own(3)[0] + first.astype(F32), own(3)[1]], axis=1).astype(BF16)
    backward = jnp.concatenate([own(5)[0], own(5)[1] + second.astype(F32)], axis=1).astype(BF16)
    yield forward, backward
    for step in range(2):
        mine, theirs = jnp.concatenate(own(2 - step), axis=1), jnp.concatenate(own(6 + step), axis=1)
        forward = (mine + lax.ppermute(forward, "col", FORWARD).astype(F32)).astype(BF16)
        backward = (theirs + lax.ppermute(backward, "col", BACKWARD).astype(F32)).astype(BF16)
        yield forward, backward
    forward = lax.ppermute(forward, "col", FORWARD).astype(F32)
    backward = lax.ppermute(backward, "col", BACKWARD).astype(F32)
    yield (jnp.concatenate(own(0), axis=1) + forward + backward).astype(BF16)


def plain_scatter(left, right):
    for _ in range(4):
        yield ()
    partial = jnp.concatenate([left, right], axis=1)
    yield lax.psum_scatter(partial, "col", scatter_dimension=0, tiled=True).astype(BF16)


def body(ring, tokens, cotangent, gate_weight, up_weight, down_weight, gate_mask, up_mask, down_mask):
    gather, scatter = (ring_gather, ring_scatter) if ring else (plain_gather, plain_scatter)

    def other_row(x):
        return lax.ppermute(x, "row", [(0, 1), (1, 0)]).astype(F32)

    features = gather(tokens, [])
    features, cotangent = lax.optimization_barrier((features, cotangent))
    arrived = []
    shard_rows = gather(cotangent, arrived)
    gate_own, gate_sent = pre_activation(features, gate_weight, gate_mask)
    up_own, up_sent = pre_activation(features, up_weight, up_mask, [gate_sent, *arrived[0]])
    gate_pre = gate_own + other_row(gate_sent)
    up_pre = up_own + other_row(up_sent)
    sigmoid_gate = jax.nn.sigmoid(gate_pre)
    activated = gate_pre * sigmoid_gate
    hidden = (activated * up_pre).astype(BF16)

    halves = tokens.shape[1] // (4 * TILE)
    left = output_partial(hidden, down_weight, down_mask, 0, halves, arrived[1])
    right = output_partial(hidden, down_weight, down_mask, halves, halves, [left, *arrived[2]])
    out_steps = scatter(left, right)

    tiles = hidden.shape[1] // TILE
    cuts = [(0, tiles // 2), (tiles // 2, tiles - tiles // 2)] if tiles > 1 else [(0, 1)]
    grads = []
    for first, count in cuts:
        own = hidden_gradient(shard_rows, down_weight, down_mask, first, count, next(out_steps))
        grads.append(own + other_row(own))
    for _ in range(2 - len(cuts)):
        next(out_steps)
    hidden_grad = jnp.concatenate(grads, axis=1)
    gate_delta = (hidden_grad * up_pre * sigmoid_gate * (1.0 + gate_pre * (1.0 - sigmoid_gate))).astype(BF16)
    up_delta = (hidden_grad * activated).astype(BF16)
    weights = gate_delta, up_delta, gate_weight, up_weight, gate_mask, up_mask
    left = input_partial(*weights, 0, halves, next(out_steps))
    right = input_partial(*weights, halves, halves, [left, *next(out_steps)])
    output = next(out_steps)

    in_steps = scatter(left, right)
    split = hidden.shape[1] > 2 * TILE
    down_grad = weight_grad(
        hidden, shard_rows, down_mask, [left, right, *next(in_steps)], (0, 2) if split else (0, 1)
    )
    gate_grad = weight_grad(features, gate_delta, gate_mask, next(in_steps))
    up_grad = weight_grad(features, up_delta, up_mask, next(in_steps))
    last = next(in_steps)
    if split:
        down_grad = weight_grad(hidden, shard_rows, down_mask, last, (1, 2), down_grad)
    input_grad = next(in_steps)
    return (output, input_grad, gate_grad, up_grad, down_grad)


def solution(mesh):
    in_specs = (
        P(("group", "col"), "row"),
        P(("group", "col"), "row"),
        P("row", "col"),
        P("row", "col"),
        P("col", "row"),
        P("row", "col"),
        P("row", "col"),
        P("col", "row"),
    )
    out_specs = (
        P(("group", "col"), "row"),
        P(("group", "col"), "row"),
        P(("group", "row"), "col"),
        P(("group", "row"), "col"),
        P(("group", "col"), "row"),
    )
    step = functools.partial(body, mesh.shape["col"] == 8)
    return jax.shard_map(step, mesh=mesh, in_specs=in_specs, out_specs=out_specs, check_vma=False)
```

time: 331 us -> 315 us (0.952)
  waiting for transfers between devices: 144 us -> 89.7 us
  Pallas kernels: 125 us -> 152 us
  other arithmetic: 10.2 us -> 25.7 us
    ppermute x16, waiting for transfers between devices: 76.2 us -> 33.9 us  [the longest x4 20.3 us: ring_scatter(): lax.ppermute(backward, 'col', BACKWARD).astype(F32)]
    pallas_call x6 -> x12, Pallas kernels: 125 us -> 152 us  [call(): pl.pallas_call(run, grid=(grid,), in_specs=[*in_specs] + [pl.BlockSpec(me...]
    ppermute x6, waiting for transfers between devices: 21.7 us -> 0.02 us  [ring_gather(): behind.append(lax.ppermute(behind[-1], 'col', FORWARD))]
    ppermute x6, waiting for transfers between devices: 29.8 us -> 42.7 us  [ring_gather(): ahead.append(lax.ppermute(ahead[-1], 'col', BACKWARD))]
    another operation x0 -> x6, other arithmetic: none -> 11.6 us
    ppermute x6, starting transfers between devices: 8.11 us -> 2.25 us  [ring_gather(): behind.append(lax.ppermute(behind[-1], 'col', FORWARD))]
    ppermute x2, waiting for transfers between devices: 8.35 us -> 13 us  [ring_gather(): top = lax.ppermute(behind[-1][:half], 'col', FORWARD)]
    ppermute x3 -> x4, waiting for transfers between devices: 4.36 us -> 0.01 us  [other_row(): return lax.ppermute(x, 'row', [(0, 1), (1, 0)]).astype(F32)]
  transfers between devices with their start and end apart: 35 -> 36, of which waited for: 22 -> 13; matrix products, arithmetic and copies ran while one was open for 4% -> 5% of each run, Pallas kernels for 13% -> 35%
where the time goes in v2:
time: 315 us; the launch traced here: 313 us
  Pallas kernels  152 us (48%)
  waiting for transfers between devices  89.7 us (28%)
  starting transfers between devices  36.6 us (12%)
  other arithmetic  25.7 us (8%)
  local copies, waits for them, and re-layouts  7.98 us (3%)
    pallas_call x12, Pallas kernels, call(): pl.pallas_call(run, grid=(grid,), in_specs=[*in_specs] + [pl.BlockSpec(me...  152 us
    ppermute x6, waiting for transfers between devices, ring_gather(): ahead.append(lax.ppermute(ahead[-1], 'col', BACKWARD))  42.7 us
    ppermute x4, waiting for transfers between devices, ring_scatter(): lax.ppermute(backward, 'col', BACKWARD).astype(F32)  20.3 us
    ppermute x2, waiting for transfers between devices, ring_gather(): top = lax.ppermute(behind[-1][:half], 'col', FORWARD)  13 us
    another operation x6, other arithmetic  11.6 us
    ppermute x6, starting transfers between devices, ring_gather(): ahead.append(lax.ppermute(ahead[-1], 'col', BACKWARD))  11.2 us
    ppermute x2, waiting for transfers between devices, ring_scatter(): backward = lax.ppermute(backward, 'col', BACKWARD).astype(F32)  9.39 us
    ppermute x4, starting transfers between devices, ring_scatter(): lax.ppermute(backward, 'col', BACKWARD).astype(F32)  7.2 us
  transfers between devices with their start and end apart: 36, of which 13 were waited for; matrix products, arithmetic and copies ran while one was open for 5% of the time, Pallas kernels for 35%

profile of v2, /device:TPU:0, one launch (start us, length us, event | category | flops | bytes accessed | tf_op | source)
XLA Modules:
  0.0 313.0 jit_solution(17509962306892752092)
XLA Ops:
  0.6 3.0 collective-permute-start
  3.8 12.1 %collective-permute-done = bf16[64,4096]{1,0:T(8,128)(2,1)S(1)} collective-permute-done((bf16[64,4096]{1,0:T(8,128)(2,1)}, bf16[64,4096]{1,0:T(8,128)(2,1)S(1)}, u32[]{:S(2)}, u32[]{:S(2)}) %collective-permute-start) | collective-permute-done | bytes 524320 | tf_op jit(solution)/shard_map/ppermute | solution.py:170
  15.8 1.7 collective-permute-start.1
  17.9 0.8 copy.14.refs_2_.refs_4_
  18.6 0.8 copy.15.refs_2_.refs_5_
  19.4 1.1 constant_dynamic-update-slice_fusion.8
  20.5 8.4 %collective-permute-done.1 = bf16[64,4096]{1,0:T(8,128)(2,1)S(1)} collective-permute-done((bf16[64,4096]{1,0:T(8,128)(2,1)S(1)}, bf16[64,4096]{1,0:T(8,128)(2,1)S(1)}, u32[]{:S(2)}, u32[]{:S(2)}) %collective-permute-start.1) | collective-permute-done | bytes 524320 | tf_op jit(solution)/shard_map/ppermute | solution.py:170
  29.0 1.3 collective-permute-start.2
  30.3 0.7 collective-permute-start.5
  31.1 10.1 %collective-permute-done.2 = bf16[64,4096]{1,0:T(8,128)(2,1)S(1)} collective-permute-done((bf16[64,4096]{1,0:T(8,128)(2,1)S(1)}, bf16[64,4096]{1,0:T(8,128)(2,1)S(1)}, u32[]{:S(2)}, u32[]{:S(2)}) %collective-permute-start.2) | collective-permute-done | bytes 524320 | tf_op jit(solution)/shard_map/ppermute | solution.py:170
  41.2 1.2 collective-permute-start.7
  42.4 0.9 collective-permute-start.6
  43.4 5.5 %collective-permute-done.6 = bf16[32,4096]{1,0:T(8,128)(2,1)S(1)} collective-permute-done((bf16[32,4096]{1,0:T(8,128)(2,1)S(1)}, bf16[32,4096]{1,0:T(8,128)(2,1)S(1)}, u32[]{:S(2)}, u32[]{:S(2)}) %collective-permute-start.6) | collective-permute-done | bytes 262176 | tf_op jit(solution)/shard_map/ppermute | solution.py:172
  49.0 1.6 collective-permute-start.10
  51.1 17.0 %shard_map.119 = (f32[512,2048]{1,0:T(8,128)}, bf16[512,2048]{1,0:T(8,128)(2,1)}) custom-call(bf16[512,4096]{1,0:T(8,128)(2,1)} %copy-done.21, bf16[4096,2048]{1,0:T(8,128)(2,1)} %refs_2_.17, s32[32,16]{1,0:T(8,128)S(1)} %copy.14.refs_2_.refs_4_), custom_call_target="tpu_custom_call" | custom-call | flops 8589934592 | bytes 27265024 | tf_op jit(solution)/shard_map/pallas_call | solution.py:44
  68.2 1.6 collective-permute-start.13
  70.2 17.0 %shard_map.120 = (f32[512,2048]{1,0:T(8,128)}, bf16[512,2048]{1,0:T(8,128)(2,1)}) custom-call(bf16[512,4096]{1,0:T(8,128)(2,1)} %copy-done.21, bf16[4096,2048]{1,0:T(8,128)(2,1)} %refs_3_.3, s32[32,16]{1,0:T(8,128)S(1)} %copy.15.refs_2_.refs_5_, bf16[512,2048]{1,0:T(8,128)(2,1)} %get-tuple-element.13.refs_3_, ...), custom_call_target="tpu_custom_call" | custom-call | flops 8589934592 | bytes 27265024 | tf_op jit(solution)/shard_map/pallas_call | solution.py:44
  87.4 1.9 collective-permute-start.15
  89.5 12.2 %collective-permute-done.15.refs_5_ = bf16[64,4096]{1,0:T(8,128)(2,1)S(1)} collective-permute-done((bf16[64,4096]{1,0:T(8,128)(2,1)S(1)}, bf16[64,4096]{1,0:T(8,128)(2,1)S(1)}, u32[]{:S(2)}, u32[]{:S(2)}) %collective-permute-start.15) | collective-permute-done | bytes 524320 | tf_op jit(solution)/shard_map/ppermute | solution.py:170
  101.7 1.8 collective-permute-start.25
  103.9 7.5 %collective-permute-done.24 = bf16[32,4096]{1,0:T(8,128)(2,1)S(1)} collective-permute-done((bf16[32,4096]{1,0:T(8,128)(2,1)S(1)}, bf16[32,4096]{1,0:T(8,128)(2,1)S(1)}, u32[]{:S(2)}, u32[]{:S(2)}) %collective-permute-start.24) | collective-permute-done | bytes 262176 | tf_op jit(solution)/shard_map/ppermute | solution.py:172
  111.7 3.1 %multiply_convert_fusion.2.refs_0_ = bf16[512,2048]{1,0:T(8,128)(2,1)} fusion(f32[512,2048]{1,0:T(8,128)S(1)} %copy-done.8, bf16[512,2048]{1,0:T(8,128)(2,1)S(1)} %collective-permute-done.11, f32[512,2048]{1,0:T(8,128)S(1)} %copy-done.6, bf16[512,2048]{1,0:T(8,128)(2,1)S(1)} %collective-permute-done.8), kind=kLoop, calls=%fused_computation.3 | loop fusion | flops 10485760 | bytes 14680064 | tf_op jit(solution)/shard_map/convert_element_type | solution.py:227
  114.8 9.6 %shard_map.121.refs_3_ = f32[512,2048]{1,0:T(8,128)} custom-call(bf16[512,2048]{1,0:T(8,128)(2,1)} %multiply_convert_fusion.2.refs_0_, bf16[2048,4096]{1,0:T(8,128)(2,1)} %refs_1_.11, s32[16,32]{1,0:T(8,128)S(1)} %copy-done, bf16[64,4096]{1,0:T(8,128)(2,1)S(1)} %collective-permute-done.12.refs_3_, bf16[64,4096]{1,0:T(8,128)(2,1)S(1)} %collective-permute-done.13.refs_4_), custom_call_target="tpu_custom_call" | custom-call | flops 4294967296 | bytes 23070720 | tf_op jit(solution)/shard_map/pallas_call | solution.py:44
  124.5 2.5 convert.32
  127.0 0.7 fusion.21
  127.7 9.8 %shard_map.122 = f32[512,2048]{1,0:T(8,128)} custom-call(bf16[512,2048]{1,0:T(8,128)(2,1)} %multiply_convert_fusion.2.refs_0_, bf16[2048,4096]{1,0:T(8,128)(2,1)} %refs_1_.11, s32[16,32]{1,0:T(8,128)S(1)} %copy-done, f32[512,2048]{1,0:T(8,128)} %shard_map.121.refs_3_, bf16[64,4096]{1,0:T(8,128)(2,1)S(1)} %collective-permute-done.14.refs_4_, ...), custom_call_target="tpu_custom_call" | custom-call | flops 4294967296 | bytes 23070720 | tf_op jit(solution)/shard_map/pallas_call | solution.py:44
  137.6 2.5 convert.34
  140.1 0.8 fusion.22
  140.8 2.0 collective-permute-start.20
  142.8 10.0 %shard_map.123 = f32[512,1024]{1,0:T(8,128)} custom-call(bf16[512,4096]{1,0:T(8,128)(2,1)} %copy-done.2, bf16[2048,4096]{1,0:T(8,128)(2,1)} %refs_1_.11, s32[16,32]{1,0:T(8,128)S(1)} %copy-done, bf16[64,2048]{1,0:T(8,128)(2,1)S(1)} %get-tuple-element.47.refs_3_, bf16[64,2048]{1,0:T(8,128)(2,1)S(1)} %get-tuple-element.50.refs_4_), custom_call_target="tpu_custom_call" | custom-call | flops 4294967296 | bytes 23070720 | tf_op jit(solution)/shard_map/pallas_call | solution.py:44
  152.9 1.5 fusion.18
  154.4 2.1 collective-permute-start.21
  156.5 1.3 fusion.16
  158.1 10.0 %shard_map.124 = f32[512,1024]{1,0:T(8,128)} custom-call(bf16[512,4096]{1,0:T(8,128)(2,1)} %copy-done.2, bf16[2048,4096]{1,0:T(8,128)(2,1)} %refs_1_.11, s32[16,32]{1,0:T(8,128)S(1)} %copy-done, bf16[64,4096]{1,0:T(8,128)(2,1)S(1)} %pad_maximum_fusion.1.refs_3_, bf16[64,4096]{1,0:T(8,128)(2,1)S(1)} %pad_maximum_fusion.2.refs_4_), custom_call_target="tpu_custom_call" | custom-call | flops 4294967296 | bytes 23070720 | tf_op jit(solution)/shard_map/pallas_call | solution.py:44
  168.9 2.1 collective-permute-start.22
  170.9 1.2 collective-permute-done.17
  172.6 10.1 %collective-permute-done.22 = bf16[64,4096]{1,0:T(8,128)(2,1)S(1)} collective-permute-done((bf16[64,4096]{1,0:T(8,128)(2,1)S(1)}, bf16[64,4096]{1,0:T(8,128)(2,1)S(1)}, u32[]{:S(2)}, u32[]{:S(2)}) %collective-permute-start.22) | collective-permute-done | bytes 524320 | tf_op jit(solution)/shard_map/ppermute | solution.py:197
  182.7 2.0 collective-permute-start.23
  184.8 0.8 collective-permute-done.18
  186.3 9.4 %collective-permute-done.23 = bf16[64,4096]{1,0:T(8,128)(2,1)S(1)} collective-permute-done((bf16[64,4096]{1,0:T(8,128)(2,1)S(1)}, bf16[64,4096]{1,0:T(8,128)(2,1)S(1)}, u32[]{:S(2)}, u32[]{:S(2)}) %collective-permute-start.23) | collective-permute-done | bytes 524320 | tf_op jit(solution)/shard_map/ppermute | solution.py:200
  195.7 2.3 collective-permute-done.19
  198.0 1.0 fusion.2
  198.9 2.0 add.77
  201.9 1.4 copy-done.7
  204.0 3.9 %multiply_convert_fusion = (bf16[512,2048]{1,0:T(8,128)(2,1)}, bf16[512,2048]{1,0:T(8,128)(2,1)}) fusion(f32[512,1024]{1,0:T(8,128)S(1)} %add.78, f32[512,1024]{1,0:T(8,128)S(1)} %add.77, f32[512,2048]{1,0:T(8,128)S(1)} %copy-done.7, bf16[512,2048]{1,0:T(8,128)(2,1)S(1)} %collective-permute-done.8, f32[512,2048]{1,0:T(8,128)S(1)} %copy-done.9, ...), kind=kLoop, calls=%fused_computation.1 | loop fusion | flops 18874368 | bytes 20971520 | tf_op jit(solution)/shard_map/convert_element_type | solution.py:244
  207.9 15.7 %shard_map.125.refs_6_.refs_3_ = f32[512,2048]{1,0:T(8,128)} custom-call(bf16[512,2048]{1,0:T(8,128)(2,1)} %get-tuple-element.18.refs_0_.refs_1_, bf16[512,2048]{1,0:T(8,128)(2,1)} %get-tuple-element.17.refs_1_, bf16[4096,2048]{1,0:T(8,128)(2,1)} %refs_2_.17, bf16[4096,2048]{1,0:T(8,128)(2,1)} %refs_3_.3, s32[32,16]{1,0:T(8,128)S(1)} %copy.14.refs_2_.refs_4_, ...), custom_call_target="tpu_custom_call" | custom-call | flops 8589934592 | bytes 41947136 | tf_op jit(solution)/shard_map/pallas_call | solution.py:44
  223.6 2.5 convert.36
  226.1 15.8 %shard_map.126.refs_4_ = f32[512,2048]{1,0:T(8,128)} custom-call(bf16[512,2048]{1,0:T(8,128)(2,1)} %get-tuple-element.18.refs_0_.refs_1_, bf16[512,2048]{1,0:T(8,128)(2,1)} %get-tuple-element.17.refs_1_, bf16[4096,2048]{1,0:T(8,128)(2,1)} %refs_2_.17, bf16[4096,2048]{1,0:T(8,128)(2,1)} %refs_3_.3, s32[32,16]{1,0:T(8,128)S(1)} %copy.14.refs_2_.refs_4_, ...), custom_call_target="tpu_custom_call" | custom-call | flops 8589934592 | bytes 41947136 | tf_op jit(solution)/shard_map/pallas_call | solution.py:44
  241.9 1.0 collective-permute-start.28
  242.9 2.5 convert.38
  245.5 1.1 collective-permute-start.32
  246.6 9.3 %shard_map.129.refs_5_ = bf16[2048,4096]{1,0:T(8,128)(2,1)} custom-call(bf16[512,2048]{1,0:T(8,128)(2,1)} %multiply_convert_fusion.2.refs_0_, bf16[512,4096]{1,0:T(8,128)(2,1)} %copy-done.2, s32[16,32]{1,0:T(8,128)S(1)} %copy-done, f32[512,2048]{1,0:T(8,128)} %shard_map.125.refs_6_.refs_3_, f32[512,2048]{1,0:T(8,128)} %shard_map.126.refs_4_, ...), custom_call_target="tpu_custom_call" | custom-call | flops 4294967296 | bytes 23070720 | tf_op jit(solution)/shard_map/pallas_call | solution.py:44
  256.3 1.1 collective-permute-start.29
  257.4 0.7 copy-done.3
  258.4 1.7 collective-permute-start.33
  260.1 14.1 %shard_map.127 = bf16[4096,2048]{1,0:T(8,128)(2,1)} custom-call(bf16[512,4096]{1,0:T(8,128)(2,1)} %copy-done.21, bf16[512,2048]{1,0:T(8,128)(2,1)} %get-tuple-element.18.refs_0_.refs_1_, s32[32,16]{1,0:T(8,128)S(1)} %copy.14.refs_2_.refs_4_, bf16[64,4096]{1,0:T(8,128)(2,1)S(1)} %pad_maximum_fusion.3.refs_3_, bf16[64,4096]{1,0:T(8,128)(2,1)S(1)} %pad_maximum_fusion.4.refs_4_), custom_call_target="tpu_custom_call" | custom-call | flops 8589934592 | bytes 23070720 | tf_op jit(solution)/shard_map/pallas_call | solution.py:44
  274.3 1.4 collective-permute-start.34
  275.8 0.8 collective-permute-start.30
  276.6 9.8 %collective-permute-done.34 = bf16[64,4096]{1,0:T(8,128)(2,1)S(1)} collective-permute-done((bf16[64,4096]{1,0:T(8,128)(2,1)S(1)}, bf16[64,4096]{1,0:T(8,128)(2,1)S(1)}, u32[]{:S(2)}, u32[]{:S(2)}) %collective-permute-start.34) | collective-permute-done | bytes 524320 | tf_op jit(solution)/shard_map/ppermute | solution.py:197
  286.4 1.4 collective-permute-start.35
  287.9 0.8 collective-permute-start.31
  288.7 14.1 %shard_map.128 = bf16[4096,2048]{1,0:T(8,128)(2,1)} custom-call(bf16[512,4096]{1,0:T(8,128)(2,1)} %copy-done.21, bf16[512,2048]{1,0:T(8,128)(2,1)} %get-tuple-element.17.refs_1_, s32[32,16]{1,0:T(8,128)S(1)} %copy.15.refs_2_.refs_5_, bf16[64,4096]{1,0:T(8,128)(2,1)S(1)} %fusion.10.refs_3_, bf16[64,4096]{1,0:T(8,128)(2,1)S(1)} %fusion.12.refs_4_), custom_call_target="tpu_custom_call" | custom-call | flops 8589934592 | bytes 23070720 | tf_op jit(solution)/shard_map/pallas_call | solution.py:44
  302.8 9.2 %shard_map.130 = bf16[2048,4096]{1,0:T(8,128)(2,1)} custom-call(bf16[512,2048]{1,0:T(8,128)(2,1)} %multiply_convert_fusion.2.refs_0_, bf16[512,4096]{1,0:T(8,128)(2,1)} %copy-done.2, s32[16,32]{1,0:T(8,128)S(1)} %copy-done, bf16[64,4096]{1,0:T(8,128)(2,1)S(1)} %fusion.9.refs_3_, ...), custom_call_target="tpu_custom_call", output_to_operand_aliasing={{}: (5, {})} | custom-call | flops 4294967296 | bytes 23070720 | tf_op jit(solution)/shard_map/pallas_call | solution.py:44
  312.0 1.0 fusion.8
  (118 shorter events, 7.7 us)
Async XLA Ops:
  0.6 15.2 %collective-permute-start = (bf16[64,4096]{1,0:T(8,128)(2,1)}, bf16[64,4096]{1,0:T(8,128)(2,1)S(1)}, u32[]{:S(2)}, u32[]{:S(2)}) collective-permute-start(bf16[64,4096]{1,0:T(8,128)(2,1)} %param.8), channel_id=1, source_target_pairs={{2,0},{4,2},{6,4},{7,6},{5,7},{3,5},{1,3},{0,1},{10,8},{12,10},{14... | collective-permute-start | bytes 1572872 | tf_op jit(solution)/shard_map/ppermute | solution.py:170
  3.6 13.9 %collective-permute-start.3 = (bf16[64,4096]{1,0:T(8,128)(2,1)}, bf16[64,4096]{1,0:T(8,128)(2,1)S(1)}, u32[]{:S(2)}, u32[]{:S(2)}) collective-permute-start(bf16[64,4096]{1,0:T(8,128)(2,1)} %param.8), channel_id=1, source_target_pairs={{0,2},{2,4},{4,6},{6,7},{7,5},{5,3},{3,1},{1,0},{8,10},{10,12},{12... | collective-permute-start | bytes 1572872 | tf_op jit(solution)/shard_map/ppermute | solution.py:169
  15.8 13.1 %collective-permute-start.1 = (bf16[64,4096]{1,0:T(8,128)(2,1)S(1)}, bf16[64,4096]{1,0:T(8,128)(2,1)S(1)}, u32[]{:S(2)}, u32[]{:S(2)}) collective-permute-start(bf16[64,4096]{1,0:T(8,128)(2,1)S(1)} %collective-permute-done), channel_id=1, source_target_pairs={{2,0},{4,2},{6,4},{7,6},{5,7},{3,5},{1,3},{0,1},{10,8},{12,10},{14... | collective-permute-start | bytes 1572872 | tf_op jit(solution)/shard_map/ppermute | solution.py:170
  17.5 12.8 %collective-permute-start.4 = (bf16[64,4096]{1,0:T(8,128)(2,1)S(1)}, bf16[64,4096]{1,0:T(8,128)(2,1)S(1)}, u32[]{:S(2)}, u32[]{:S(2)}) collective-permute-start(bf16[64,4096]{1,0:T(8,128)(2,1)S(1)} %collective-permute-done.3), channel_id=1, source_target_pairs={{0,2},{2,4},{4,6},{6,7},{7,5},{5,3},{3,1},{1,0},{8,10},{10,12},{12... | collective-permute-start | bytes 1572872 | tf_op jit(solution)/shard_map/ppermute | solution.py:169
  20.5 28.5 %copy-start.20 = (bf16[64,4096]{1,0:T(8,128)(2,1)S(1)}, bf16[64,4096]{1,0:T(8,128)(2,1)}, u32[]{:S(2)}) copy-start(bf16[64,4096]{1,0:T(8,128)(2,1)} %param.9) | copy-start | bytes 1572868
  29.0 12.2 %collective-permute-start.2 = (bf16[64,4096]{1,0:T(8,128)(2,1)S(1)}, bf16[64,4096]{1,0:T(8,128)(2,1)S(1)}, u32[]{:S(2)}, u32[]{:S(2)}) collective-permute-start(bf16[64,4096]{1,0:T(8,128)(2,1)S(1)} %collective-permute-done.1), channel_id=1, source_target_pairs={{2,0},{4,2},{6,4},{7,6},{5,7},{3,5},{1,3},{0,1},{10,8},{12,10},{14... | collective-permute-start | bytes 1572872 | tf_op jit(solution)/shard_map/ppermute | solution.py:170
  30.3 12.1 %collective-permute-start.5 = (bf16[64,4096]{1,0:T(8,128)(2,1)S(1)}, bf16[64,4096]{1,0:T(8,128)(2,1)S(1)}, u32[]{:S(2)}, u32[]{:S(2)}) collective-permute-start(bf16[64,4096]{1,0:T(8,128)(2,1)S(1)} %collective-permute-done.4), channel_id=1, source_target_pairs={{0,2},{2,4},{4,6},{6,7},{7,5},{5,3},{3,1},{1,0},{8,10},{10,12},{12... | collective-permute-start | bytes 1572872 | tf_op jit(solution)/shard_map/ppermute | solution.py:169
  41.2 7.7 %collective-permute-start.7 = (bf16[32,4096]{1,0:T(8,128)(2,1)S(1)}, bf16[32,4096]{1,0:T(8,128)(2,1)S(1)}, u32[]{:S(2)}, u32[]{:S(2)}) collective-permute-start(bf16[32,4096]{1,0:T(8,128)(2,1)S(1)} %slice.153), channel_id=1, source_target_pairs={{2,0},{4,2},{6,4},{7,6},{5,7},{3,5},{1,3},{0,1},{10,8},{12,10},{14... | collective-permute-start | bytes 786440 | tf_op jit(solution)/shard_map/ppermute | solution.py:173
  42.4 6.4 %collective-permute-start.6 = (bf16[32,4096]{1,0:T(8,128)(2,1)S(1)}, bf16[32,4096]{1,0:T(8,128)(2,1)S(1)}, u32[]{:S(2)}, u32[]{:S(2)}) collective-permute-start(bf16[32,4096]{1,0:T(8,128)(2,1)S(1)} %slice.152), channel_id=1, source_target_pairs={{0,2},{2,4},{4,6},{6,7},{7,5},{5,3},{3,1},{1,0},{8,10},{10,12},{12... | collective-permute-start | bytes 786440 | tf_op jit(solution)/shard_map/ppermute | solution.py:172
  49.0 2.1 copy-start.21
  49.0 19.1 %collective-permute-start.10 = (bf16[64,4096]{1,0:T(8,128)(2,1)S(1)}, bf16[64,4096]{1,0:T(8,128)(2,1)S(1)}, u32[]{:S(2)}, u32[]{:S(2)}) collective-permute-start(bf16[64,4096]{1,0:T(8,128)(2,1)S(1)} %copy-done.20), channel_id=1, source_target_pairs={{2,0},{4,2},{6,4},{7,6},{5,7},{3,5},{1,3},{0,1},{10,8},{12,10},{14... | collective-permute-start | bytes 1572872 | tf_op jit(solution)/shard_map/ppermute | solution.py:170
  50.7 19.1 %collective-permute-start.9 = (bf16[64,4096]{1,0:T(8,128)(2,1)S(1)}, bf16[64,4096]{1,0:T(8,128)(2,1)S(1)}, u32[]{:S(2)}, u32[]{:S(2)}) collective-permute-start(bf16[64,4096]{1,0:T(8,128)(2,1)S(1)} %copy-done.20), channel_id=1, source_target_pairs={{0,2},{2,4},{4,6},{6,7},{7,5},{5,3},{3,1},{1,0},{8,10},{10,12},{12... | collective-permute-start | bytes 1572872 | tf_op jit(solution)/shard_map/ppermute | solution.py:169
  68.1 43.5 %collective-permute-start.8 = (bf16[512,2048]{1,0:T(8,128)(2,1)}, bf16[512,2048]{1,0:T(8,128)(2,1)S(1)}, u32[]{:S(2)}, u32[]{:S(2)}) collective-permute-start(bf16[512,2048]{1,0:T(8,128)(2,1)} %get-tuple-element.13.refs_3_), channel_id=1, source_target_pairs={{0,8},{8,0},{1,9},{9,1},{2,10},{10,2},{3,11},{11,3},{4,12},{12,4},... | collective-permute-start | bytes 6291464 | tf_op jit(solution)/shard_map/ppermute | solution.py:215
  68.2 19.2 %collective-permute-start.13 = (bf16[64,4096]{1,0:T(8,128)(2,1)S(1)}, bf16[64,4096]{1,0:T(8,128)(2,1)S(1)}, u32[]{:S(2)}, u32[]{:S(2)}) collective-permute-start(bf16[64,4096]{1,0:T(8,128)(2,1)S(1)} %collective-permute-done.10.refs_5_), channel_id=1, source_target_pairs={{2,0},{4,2},{6,4},{7,6},{5,7},{3,5},{1,3},{0,1},{10,8},{12,10},{14... | collective-permute-start | bytes 1572872 | tf_op jit(solution)/shard_map/ppermute | solution.py:170
  69.8 19.5 %collective-permute-start.12 = (bf16[64,4096]{1,0:T(8,128)(2,1)S(1)}, bf16[64,4096]{1,0:T(8,128)(2,1)S(1)}, u32[]{:S(2)}, u32[]{:S(2)}) collective-permute-start(bf16[64,4096]{1,0:T(8,128)(2,1)S(1)} %collective-permute-done.9.refs_4_), channel_id=1, source_target_pairs={{0,2},{2,4},{4,6},{6,7},{7,5},{5,3},{3,1},{1,0},{8,10},{10,12},{12... | collective-permute-start | bytes 1572872 | tf_op jit(solution)/shard_map/ppermute | solution.py:169
  87.3 24.4 %copy-start.6 = (f32[512,2048]{1,0:T(8,128)S(1)}, f32[512,2048]{1,0:T(8,128)}, u32[]{:S(2)}) copy-start(f32[512,2048]{1,0:T(8,128)} %get-tuple-element.12) | copy-start | bytes 12582916
  87.3 24.4 %copy-start.8 = (f32[512,2048]{1,0:T(8,128)S(1)}, f32[512,2048]{1,0:T(8,128)}, u32[]{:S(2)}) copy-start(f32[512,2048]{1,0:T(8,128)} %get-tuple-element.15) | copy-start | bytes 12582916
  87.3 24.4 %collective-permute-start.11 = (bf16[512,2048]{1,0:T(8,128)(2,1)}, bf16[512,2048]{1,0:T(8,128)(2,1)S(1)}, u32[]{:S(2)}, u32[]{:S(2)}) collective-permute-start(bf16[512,2048]{1,0:T(8,128)(2,1)} %get-tuple-element.16), channel_id=1, source_target_pairs={{0,8},{8,0},{1,9},{9,1},{2,10},{10,2},{3,11},{11,3},{4,12},{12,4},... | collective-permute-start | bytes 6291464 | tf_op jit(solution)/shard_map/ppermute | solution.py:215
  87.4 14.3 %collective-permute-start.15 = (bf16[64,4096]{1,0:T(8,128)(2,1)S(1)}, bf16[64,4096]{1,0:T(8,128)(2,1)S(1)}, u32[]{:S(2)}, u32[]{:S(2)}) collective-permute-start(bf16[64,4096]{1,0:T(8,128)(2,1)S(1)} %collective-permute-done.13.refs_4_), channel_id=1, source_target_pairs={{2,0},{4,2},{6,4},{7,6},{5,7},{3,5},{1,3},{0,1},{10,8},{12,10},{14... | collective-permute-start | bytes 1572872 | tf_op jit(solution)/shard_map/ppermute | solution.py:170
  89.3 14.2 %collective-permute-start.14 = (bf16[64,4096]{1,0:T(8,128)(2,1)S(1)}, bf16[64,4096]{1,0:T(8,128)(2,1)S(1)}, u32[]{:S(2)}, u32[]{:S(2)}) collective-permute-start(bf16[64,4096]{1,0:T(8,128)(2,1)S(1)} %collective-permute-done.12.refs_3_), channel_id=1, source_target_pairs={{0,2},{2,4},{4,6},{6,7},{7,5},{5,3},{3,1},{1,0},{8,10},{10,12},{12... | collective-permute-start | bytes 1572872 | tf_op jit(solution)/shard_map/ppermute | solution.py:169
  101.7 9.7 %collective-permute-start.25 = (bf16[32,4096]{1,0:T(8,128)(2,1)S(1)}, bf16[32,4096]{1,0:T(8,128)(2,1)S(1)}, u32[]{:S(2)}, u32[]{:S(2)}) collective-permute-start(bf16[32,4096]{1,0:T(8,128)(2,1)S(1)} %slice.171), channel_id=1, source_target_pairs={{2,0},{4,2},{6,4},{7,6},{5,7},{3,5},{1,3},{0,1},{10,8},{12,10},{14... | collective-permute-start | bytes 786440 | tf_op jit(solution)/shard_map/ppermute | solution.py:173
  103.5 7.9 %collective-permute-start.24 = (bf16[32,4096]{1,0:T(8,128)(2,1)S(1)}, bf16[32,4096]{1,0:T(8,128)(2,1)S(1)}, u32[]{:S(2)}, u32[]{:S(2)}) collective-permute-start(bf16[32,4096]{1,0:T(8,128)(2,1)S(1)} %slice.170), channel_id=1, source_target_pairs={{0,2},{2,4},{4,6},{6,7},{7,5},{5,3},{3,1},{1,0},{8,10},{10,12},{12... | collective-permute-start | bytes 786440 | tf_op jit(solution)/shard_map/ppermute | solution.py:172
  111.6 3.2 %copy-start.2 = (bf16[512,4096]{1,0:T(8,128)(2,1)}, bf16[512,4096]{1,0:T(8,128)(2,1)S(1)}, u32[]{:S(2)}) copy-start(bf16[512,4096]{1,0:T(8,128)(2,1)S(1)} %constant_dynamic-update-slice_fusion.9.refs_0_.refs_1_) | copy-start | bytes 12582916
  111.6 3.2 %copy-start.10 = (bf16[512,2048]{1,0:T(8,128)(2,1)}, bf16[512,2048]{1,0:T(8,128)(2,1)S(1)}, u32[]{:S(2)}) copy-start(bf16[512,2048]{1,0:T(8,128)(2,1)S(1)} %collective-permute-done.11) | copy-start | bytes 6291460
  111.7 3.1 %copy-start = (s32[16,32]{1,0:T(8,128)S(1)}, s32[16,32]{1,0:T(8,128)}, u32[]{:S(2)}) copy-start(s32[16,32]{1,0:T(8,128)} %refs_2_.19) | copy-start | bytes 6148
  127.7 28.8 %collective-permute-start.16 = (bf16[64,2048]{1,0:T(8,128)(2,1)S(1)}, bf16[64,2048]{1,0:T(8,128)(2,1)}, u32[]{:S(2)}, u32[]{:S(2)}) collective-permute-start(bf16[64,2048]{1,0:T(8,128)(2,1)S(1)} %get-tuple-element.47.refs_3_), channel_id=1, source_target_pairs={{0,2},{2,4},{4,6},{6,7},{7,5},{5,3},{3,1},{1,0},{8,10},{10,12},{12... | collective-permute-start | bytes 786440 | tf_op jit(solution)/shard_map/ppermute | solution.py:190
  140.8 12.1 %copy-start.5 = (f32[512,2048]{1,0:T(8,128)S(1)}, f32[512,2048]{1,0:T(8,128)}, u32[]{:S(2)}) copy-start(f32[512,2048]{1,0:T(8,128)} %shard_map.122) | copy-start | bytes 12582916
  140.8 12.1 %collective-permute-start.20 = (bf16[64,2048]{1,0:T(8,128)(2,1)S(1)}, bf16[64,2048]{1,0:T(8,128)(2,1)S(1)}, u32[]{:S(2)}, u32[]{:S(2)}) collective-permute-start(bf16[64,2048]{1,0:T(8,128)(2,1)S(1)} %get-tuple-element.50.refs_4_), channel_id=1, source_target_pairs={{2,0},{4,2},{6,4},{7,6},{5,7},{3,5},{1,3},{0,1},{10,8},{12,10},{14... | collective-permute-start | bytes 786440 | tf_op jit(solution)/shard_map/ppermute | solution.py:190
  152.9 1.5 copy-start.19
  152.9 3.6 %copy-start.4 = (f32[512,2048]{1,0:T(8,128)S(1)}, f32[512,2048]{1,0:T(8,128)}, u32[]{:S(2)}) copy-start(f32[512,2048]{1,0:T(8,128)} %shard_map.121.refs_3_) | copy-start | bytes 12582916
  152.9 46.1 %collective-permute-start.26 = (f32[512,1024]{1,0:T(8,128)}, f32[512,1024]{1,0:T(8,128)}, u32[]{:S(2)}, u32[]{:S(2)}) collective-permute-start(f32[512,1024]{1,0:T(8,128)} %shard_map.123), channel_id=1, source_target_pairs={{0,8},{8,0},{1,9},{9,1},{2,10},{10,2},{3,11},{11,3},{4,12},{12,4},... | collective-permute-start | bytes 6291464 | tf_op jit(solution)/shard_map/ppermute | solution.py:215
  154.4 3.4 %copy-start.18 = (bf16[64,2048]{1,0:T(8,128)(2,1)S(1)}, bf16[64,2048]{1,0:T(8,128)(2,1)}, u32[]{:S(2)}) copy-start(bf16[64,2048]{1,0:T(8,128)(2,1)} %get-tuple-element.49) | copy-start | bytes 786436
  154.4 14.4 %collective-permute-start.21 = (bf16[64,4096]{1,0:T(8,128)(2,1)S(1)}, bf16[64,4096]{1,0:T(8,128)(2,1)S(1)}, u32[]{:S(2)}, u32[]{:S(2)}) collective-permute-start(bf16[64,4096]{1,0:T(8,128)(2,1)S(1)} %pad_maximum_fusion.2.refs_4_), channel_id=1, source_target_pairs={{2,0},{4,2},{6,4},{7,6},{5,7},{3,5},{1,3},{0,1},{10,8},{12,10},{14... | collective-permute-start | bytes 1572872 | tf_op jit(solution)/shard_map/ppermute | solution.py:197
  157.9 10.9 %copy-start.17 = (f32[64,2048]{1,0:T(8,128)S(1)}, f32[64,2048]{1,0:T(8,128)}, u32[]{:S(2)}) copy-start(f32[64,2048]{1,0:T(8,128)} %get-tuple-element.39) | copy-start | bytes 1572868
  157.9 14.3 %copy-start.16 = (f32[64,2048]{1,0:T(8,128)S(1)}, f32[64,2048]{1,0:T(8,128)}, u32[]{:S(2)}) copy-start(f32[64,2048]{1,0:T(8,128)} %get-tuple-element.37) | copy-start | bytes 1572868
  157.9 14.3 %collective-permute-start.17 = (bf16[64,4096]{1,0:T(8,128)(2,1)S(1)}, bf16[64,4096]{1,0:T(8,128)(2,1)S(1)}, u32[]{:S(2)}, u32[]{:S(2)}) collective-permute-start(bf16[64,4096]{1,0:T(8,128)(2,1)S(1)} %pad_maximum_fusion.1.refs_3_), channel_id=1, source_target_pairs={{0,2},{2,4},{4,6},{6,7},{7,5},{5,3},{3,1},{1,0},{8,10},{10,12},{12... | collective-permute-start | bytes 1572872 | tf_op jit(solution)/shard_map/ppermute | solution.py:196
  168.2 14.5 %copy-start.15 = (f32[64,2048]{1,0:T(8,128)S(1)}, f32[64,2048]{1,0:T(8,128)}, u32[]{:S(2)}) copy-start(f32[64,2048]{1,0:T(8,128)} %get-tuple-element.40) | copy-start | bytes 1572868
  168.2 17.4 %copy-start.14 = (f32[64,2048]{1,0:T(8,128)S(1)}, f32[64,2048]{1,0:T(8,128)}, u32[]{:S(2)}) copy-start(f32[64,2048]{1,0:T(8,128)} %get-tuple-element.41) | copy-start | bytes 1572868
  168.2 32.8 %collective-permute-start.27 = (f32[512,1024]{1,0:T(8,128)}, f32[512,1024]{1,0:T(8,128)S(1)}, u32[]{:S(2)}, u32[]{:S(2)}) collective-permute-start(f32[512,1024]{1,0:T(8,128)} %shard_map.124), channel_id=1, source_target_pairs={{0,8},{8,0},{1,9},{9,1},{2,10},{10,2},{3,11},{11,3},{4,12},{12,4},... | collective-permute-start | bytes 6291464 | tf_op jit(solution)/shard_map/ppermute | solution.py:215
  168.9 13.8 %collective-permute-start.22 = (bf16[64,4096]{1,0:T(8,128)(2,1)S(1)}, bf16[64,4096]{1,0:T(8,128)(2,1)S(1)}, u32[]{:S(2)}, u32[]{:S(2)}) collective-permute-start(bf16[64,4096]{1,0:T(8,128)(2,1)S(1)} %fusion.6.refs_7_), channel_id=1, source_target_pairs={{2,0},{4,2},{6,4},{7,6},{5,7},{3,5},{1,3},{0,1},{10,8},{12,10},{14... | collective-permute-start | bytes 1572872 | tf_op jit(solution)/shard_map/ppermute | solution.py:197
  172.2 26.8 %copy-start.12 = (f32[512,1024]{1,0:T(8,128)S(1)}, f32[512,1024]{1,0:T(8,128)}, u32[]{:S(2)}) copy-start(f32[512,1024]{1,0:T(8,128)} %shard_map.123) | copy-start | bytes 6291460
  172.3 13.3 %collective-permute-start.18 = (bf16[64,4096]{1,0:T(8,128)(2,1)S(1)}, bf16[64,4096]{1,0:T(8,128)(2,1)S(1)}, u32[]{:S(2)}, u32[]{:S(2)}) collective-permute-start(bf16[64,4096]{1,0:T(8,128)(2,1)S(1)} %fusion.4.refs_6_), channel_id=1, source_target_pairs={{0,2},{2,4},{4,6},{6,7},{7,5},{5,3},{3,1},{1,0},{8,10},{10,12},{12... | collective-permute-start | bytes 1572872 | tf_op jit(solution)/shard_map/ppermute | solution.py:196
  182.7 12.9 %collective-permute-start.23 = (bf16[64,4096]{1,0:T(8,128)(2,1)S(1)}, bf16[64,4096]{1,0:T(8,128)(2,1)S(1)}, u32[]{:S(2)}, u32[]{:S(2)}) collective-permute-start(bf16[64,4096]{1,0:T(8,128)(2,1)S(1)} %fusion.5.refs_8_), channel_id=1, source_target_pairs={{2,0},{4,2},{6,4},{7,6},{5,7},{3,5},{1,3},{0,1},{10,8},{12,10},{14... | collective-permute-start | bytes 1572872 | tf_op jit(solution)/shard_map/ppermute | solution.py:200
  185.6 12.3 %collective-permute-start.19 = (bf16[64,4096]{1,0:T(8,128)(2,1)S(1)}, bf16[64,4096]{1,0:T(8,128)(2,1)S(1)}, u32[]{:S(2)}, u32[]{:S(2)}) collective-permute-start(bf16[64,4096]{1,0:T(8,128)(2,1)S(1)} %fusion.3.refs_7_), channel_id=1, source_target_pairs={{0,2},{2,4},{4,6},{6,7},{7,5},{5,3},{3,1},{1,0},{8,10},{10,12},{12... | collective-permute-start | bytes 1572872 | tf_op jit(solution)/shard_map/ppermute | solution.py:199
  198.0 3.0 copy-start.13
  198.9 3.0 copy-start.9
  200.9 2.4 copy-start.7
  200.9 3.0 copy-start.11
  241.9 14.0 %collective-permute-start.28 = (bf16[64,2048]{1,0:T(8,128)(2,1)S(1)}, bf16[64,2048]{1,0:T(8,128)(2,1)S(1)}, u32[]{:S(2)}, u32[]{:S(2)}) collective-permute-start(bf16[64,2048]{1,0:T(8,128)(2,1)S(1)} %get-tuple-element.43.refs_5_), channel_id=1, source_target_pairs={{0,2},{2,4},{4,6},{6,7},{7,5},{5,3},{3,1},{1,0},{8,10},{10,12},{12... | collective-permute-start | bytes 786440 | tf_op jit(solution)/shard_map/ppermute | solution.py:190
  245.5 10.4 %copy-start.1 = (f32[512,2048]{1,0:T(8,128)S(1)}, f32[512,2048]{1,0:T(8,128)}, u32[]{:S(2)}) copy-start(f32[512,2048]{1,0:T(8,128)} %shard_map.125.refs_6_.refs_3_) | copy-start | bytes 12582916
  245.5 11.9 %collective-permute-start.32 = (bf16[64,2048]{1,0:T(8,128)(2,1)S(1)}, bf16[64,2048]{1,0:T(8,128)(2,1)S(1)}, u32[]{:S(2)}, u32[]{:S(2)}) collective-permute-start(bf16[64,2048]{1,0:T(8,128)(2,1)S(1)} %get-tuple-element.46.refs_6_), channel_id=1, source_target_pairs={{2,0},{4,2},{6,4},{7,6},{5,7},{3,5},{1,3},{0,1},{10,8},{12,10},{14... | collective-permute-start | bytes 786440 | tf_op jit(solution)/shard_map/ppermute | solution.py:190
  255.9 2.2 copy-start.3
  256.3 19.4 %collective-permute-start.29 = (bf16[64,4096]{1,0:T(8,128)(2,1)S(1)}, bf16[64,4096]{1,0:T(8,128)(2,1)S(1)}, u32[]{:S(2)}, u32[]{:S(2)}) collective-permute-start(bf16[64,4096]{1,0:T(8,128)(2,1)S(1)} %pad_maximum_fusion.3.refs_3_), channel_id=1, source_target_pairs={{0,2},{2,4},{4,6},{6,7},{7,5},{5,3},{3,1},{1,0},{8,10},{10,12},{12... | collective-permute-start | bytes 1572872 | tf_op jit(solution)/shard_map/ppermute | solution.py:196
  258.4 15.9 %collective-permute-start.33 = (bf16[64,4096]{1,0:T(8,128)(2,1)S(1)}, bf16[64,4096]{1,0:T(8,128)(2,1)S(1)}, u32[]{:S(2)}, u32[]{:S(2)}) collective-permute-start(bf16[64,4096]{1,0:T(8,128)(2,1)S(1)} %pad_maximum_fusion.4.refs_4_), channel_id=1, source_target_pairs={{2,0},{4,2},{6,4},{7,6},{5,7},{3,5},{1,3},{0,1},{10,8},{12,10},{14... | collective-permute-start | bytes 1572872 | tf_op jit(solution)/shard_map/ppermute | solution.py:197
  274.3 12.0 %collective-permute-start.34 = (bf16[64,4096]{1,0:T(8,128)(2,1)S(1)}, bf16[64,4096]{1,0:T(8,128)(2,1)S(1)}, u32[]{:S(2)}, u32[]{:S(2)}) collective-permute-start(bf16[64,4096]{1,0:T(8,128)(2,1)S(1)} %fusion.12.refs_4_), channel_id=1, source_target_pairs={{2,0},{4,2},{6,4},{7,6},{5,7},{3,5},{1,3},{0,1},{10,8},{12,10},{14... | collective-permute-start | bytes 1572872 | tf_op jit(solution)/shard_map/ppermute | solution.py:197
  275.8 12.0 %collective-permute-start.30 = (bf16[64,4096]{1,0:T(8,128)(2,1)S(1)}, bf16[64,4096]{1,0:T(8,128)(2,1)S(1)}, u32[]{:S(2)}, u32[]{:S(2)}) collective-permute-start(bf16[64,4096]{1,0:T(8,128)(2,1)S(1)} %fusion.10.refs_3_), channel_id=1, source_target_pairs={{0,2},{2,4},{4,6},{6,7},{7,5},{5,3},{3,1},{1,0},{8,10},{10,12},{12... | collective-permute-start | bytes 1572872 | tf_op jit(solution)/shard_map/ppermute | solution.py:196
  286.4 25.6 %collective-permute-start.35 = (bf16[64,4096]{1,0:T(8,128)(2,1)S(1)}, bf16[64,4096]{1,0:T(8,128)(2,1)S(1)}, u32[]{:S(2)}, u32[]{:S(2)}) collective-permute-start(bf16[64,4096]{1,0:T(8,128)(2,1)S(1)} %fusion.11.refs_4_), channel_id=1, source_target_pairs={{2,0},{4,2},{6,4},{7,6},{5,7},{3,5},{1,3},{0,1},{10,8},{12,10},{14... | collective-permute-start | bytes 1572872 | tf_op jit(solution)/shard_map/ppermute | solution.py:200
  287.9 24.1 %collective-permute-start.31 = (bf16[64,4096]{1,0:T(8,128)(2,1)S(1)}, bf16[64,4096]{1,0:T(8,128)(2,1)S(1)}, u32[]{:S(2)}, u32[]{:S(2)}) collective-permute-start(bf16[64,4096]{1,0:T(8,128)(2,1)S(1)} %fusion.9.refs_3_), channel_id=1, source_target_pairs={{0,2},{2,4},{4,6},{6,7},{7,5},{5,3},{3,1},{1,0},{8,10},{10,12},{12... | collective-permute-start | bytes 1572872 | tf_op jit(solution)/shard_map/ppermute | solution.py:199

commit v3 on v2

--- a/solution.py
+++ b/solution.py
@@ -185,7 +185,8 @@
     def own(j):
         return left[j * rows:(j + 1) * rows], right[j * rows:(j + 1) * rows]
 
-    sent = own(4)[0].astype(BF16), own(4)[1].astype(BF16)
+    low, high = lax.optimization_barrier(own(4))
+    sent = low.astype(BF16), high.astype(BF16)
     yield sent
     first, second = lax.ppermute(sent[0], "col", FORWARD), lax.ppermute(sent[1], "col", BACKWARD)
     forward = jnp.concatenate([own(3)[0] + first.astype(F32), own(3)[1]], axis=1).astype(BF16)
@@ -195,7 +196,9 @@
         mine, theirs = jnp.concatenate(own(2 - step), axis=1), jnp.concatenate(own(6 + step), axis=1)
         forward = (mine + lax.ppermute(forward, "col", FORWARD).astype(F32)).astype(BF16)
         backward = (theirs + lax.ppermute(backward, "col", BACKWARD).astype(F32)).astype(BF16)
-        yield forward, backward
+        gate = yield forward, backward
+        if gate is not None:
+            forward, backward, _ = lax.optimization_barrier((forward, backward, gate))
     forward = lax.ppermute(forward, "col", FORWARD).astype(F32)
     backward = lax.ppermute(backward, "col", BACKWARD).astype(F32)
     yield (jnp.concatenate(own(0), axis=1) + forward + backward).astype(BF16)
@@ -243,8 +246,9 @@
     gate_delta = (hidden_grad * up_pre * sigmoid_gate * (1.0 + gate_pre * (1.0 - sigmoid_gate))).astype(BF16)
     up_delta = (hidden_grad * activated).astype(BF16)
     weights = gate_delta, up_delta, gate_weight, up_weight, gate_mask, up_mask
-    left = input_partial(*weights, 0, halves, next(out_steps))
-    right = input_partial(*weights, halves, halves, [left, *next(out_steps)])
+    next(out_steps)
+    left = input_partial(*weights, 0, halves)
+    right = input_partial(*weights, halves, halves, [left, *out_steps.send(gate_delta)])
     output = next(out_steps)
 
     in_steps = scatter(left, right)

time: 315 us -> 305 us (0.968)
  waiting for transfers between devices: 89.7 us -> 78.2 us
  local copies, waits for them, and re-layouts: 7.98 us -> 12.8 us
    ppermute x4, waiting for transfers between devices: 1.97 us -> 22.4 us  [ring_scatter(): lax.ppermute(forward, 'col', FORWARD).astype(F32)]
    ppermute x4, waiting for transfers between devices: 20.3 us -> 0.01 us  [ring_scatter(): lax.ppermute(backward, 'col', BACKWARD).astype(F32)]
    another operation x6 -> x1, other arithmetic: 11.6 us -> 1.19 us
    ppermute x2, waiting for transfers between devices: 9.39 us -> 0.01 us  [ring_scatter(): backward = lax.ppermute(backward, 'col', BACKWARD).astype(F32)]
    slice x4, local copies, waits for them, and re-layouts: 1.58 us -> 5.75 us  [own(): return (left[j * rows:(j + 1) * rows], right[j * rows:(j + 1) * rows])]
    slice x2 -> x3, other arithmetic: 1.7 us -> 5.1 us  [own(): return (left[j * rows:(j + 1) * rows], right[j * rows:(j + 1) * rows])]
    unnamed x62 -> x58, local copies, waits for them, and re-layouts: 6.26 us -> 6.88 us
  transfers between devices with their start and end apart: 36 -> 36, of which waited for: 13 -> 8; matrix products, arithmetic and copies ran while one was open for 5% -> 6% of each run, Pallas kernels for 35% -> 44%
where the time goes in v3:
time: 305 us; the launch traced here: 303 us
  Pallas kernels  152 us (50%)
  waiting for transfers between devices  78.2 us (26%)
  starting transfers between devices  35 us (11%)
  other arithmetic  23.9 us (8%)
  local copies, waits for them, and re-layouts  12.8 us (4%)
    pallas_call x12, Pallas kernels, call(): pl.pallas_call(run, grid=(grid,), in_specs=[*in_specs] + [pl.BlockSpec(me...  152 us
    ppermute x6, waiting for transfers between devices, ring_gather(): ahead.append(lax.ppermute(ahead[-1], 'col', BACKWARD))  42.7 us
    ppermute x4, waiting for transfers between devices, ring_scatter(): lax.ppermute(forward, 'col', FORWARD).astype(F32)  22.4 us
    ppermute x2, waiting for transfers between devices, ring_gather(): top = lax.ppermute(behind[-1][:half], 'col', FORWARD)  13 us
    ppermute x6, starting transfers between devices, ring_gather(): ahead.append(lax.ppermute(ahead[-1], 'col', BACKWARD))  11.2 us
    ppermute x4, starting transfers between devices, ring_scatter(): lax.ppermute(backward, 'col', BACKWARD).astype(F32)  7.52 us
    unnamed x58, local copies, waits for them, and re-layouts  6.88 us
  transfers between devices with their start and end apart: 36, of which 8 were waited for; matrix products, arithmetic and copies ran while one was open for 6% of the time, Pallas kernels for 44%

profile of v3, /device:TPU:0, one launch (start us, length us, event | category | flops | bytes accessed | tf_op | source)
XLA Modules:
  0.0 302.8 jit_solution(4883516782088981650)
XLA Ops:
  0.6 3.0 collective-permute-start
  3.8 12.1 %collective-permute-done = bf16[64,4096]{1,0:T(8,128)(2,1)S(1)} collective-permute-done((bf16[64,4096]{1,0:T(8,128)(2,1)}, bf16[64,4096]{1,0:T(8,128)(2,1)S(1)}, u32[]{:S(2)}, u32[]{:S(2)}) %collective-permute-start) | collective-permute-done | bytes 524320 | tf_op jit(solution)/shard_map/ppermute | solution.py:170
  15.8 1.7 collective-permute-start.1
  17.5 0.4 collective-permute-start.4
  17.9 0.8 copy.14.refs_2_.refs_4_
  18.6 0.8 copy.15.refs_2_.refs_5_
  19.4 1.1 constant_dynamic-update-slice_fusion.8
  20.5 8.4 %collective-permute-done.1 = bf16[64,4096]{1,0:T(8,128)(2,1)S(1)} collective-permute-done((bf16[64,4096]{1,0:T(8,128)(2,1)S(1)}, bf16[64,4096]{1,0:T(8,128)(2,1)S(1)}, u32[]{:S(2)}, u32[]{:S(2)}) %collective-permute-start.1) | collective-permute-done | bytes 524320 | tf_op jit(solution)/shard_map/ppermute | solution.py:170
  29.0 1.3 collective-permute-start.2
  30.3 0.7 collective-permute-start.5
  31.1 10.1 %collective-permute-done.2 = bf16[64,4096]{1,0:T(8,128)(2,1)S(1)} collective-permute-done((bf16[64,4096]{1,0:T(8,128)(2,1)S(1)}, bf16[64,4096]{1,0:T(8,128)(2,1)S(1)}, u32[]{:S(2)}, u32[]{:S(2)}) %collective-permute-start.2) | collective-permute-done | bytes 524320 | tf_op jit(solution)/shard_map/ppermute | solution.py:170
  41.2 1.2 collective-permute-start.7
  42.4 0.9 collective-permute-start.6
  43.4 5.5 %collective-permute-done.6 = bf16[32,4096]{1,0:T(8,128)(2,1)S(1)} collective-permute-done((bf16[32,4096]{1,0:T(8,128)(2,1)S(1)}, bf16[32,4096]{1,0:T(8,128)(2,1)S(1)}, u32[]{:S(2)}, u32[]{:S(2)}) %collective-permute-start.6) | collective-permute-done | bytes 262176 | tf_op jit(solution)/shard_map/ppermute | solution.py:172
  49.0 1.6 collective-permute-start.10
  50.7 0.4 collective-permute-start.9
  51.1 17.0 %shard_map.119 = (f32[512,2048]{1,0:T(8,128)}, bf16[512,2048]{1,0:T(8,128)(2,1)}) custom-call(bf16[512,4096]{1,0:T(8,128)(2,1)} %copy-done.19, bf16[4096,2048]{1,0:T(8,128)(2,1)} %refs_2_.17, s32[32,16]{1,0:T(8,128)S(1)} %copy.14.refs_2_.refs_4_), custom_call_target="tpu_custom_call" | custom-call | flops 8589934592 | bytes 27265024 | tf_op jit(solution)/shard_map/pallas_call | solution.py:44
  68.2 1.6 collective-permute-start.13
  69.8 0.5 collective-permute-start.12
  70.2 17.0 %shard_map.120 = (f32[512,2048]{1,0:T(8,128)}, bf16[512,2048]{1,0:T(8,128)(2,1)}) custom-call(bf16[512,4096]{1,0:T(8,128)(2,1)} %copy-done.19, bf16[4096,2048]{1,0:T(8,128)(2,1)} %refs_3_.3, s32[32,16]{1,0:T(8,128)S(1)} %copy.15.refs_2_.refs_5_, bf16[512,2048]{1,0:T(8,128)(2,1)} %get-tuple-element.19.refs_3_, ...), custom_call_target="tpu_custom_call" | custom-call | flops 8589934592 | bytes 27265024 | tf_op jit(solution)/shard_map/pallas_call | solution.py:44
  87.3 1.9 collective-permute-start.15
  89.5 12.2 %collective-permute-done.15.refs_5_ = bf16[64,4096]{1,0:T(8,128)(2,1)S(1)} collective-permute-done((bf16[64,4096]{1,0:T(8,128)(2,1)S(1)}, bf16[64,4096]{1,0:T(8,128)(2,1)S(1)}, u32[]{:S(2)}, u32[]{:S(2)}) %collective-permute-start.15) | collective-permute-done | bytes 524320 | tf_op jit(solution)/shard_map/ppermute | solution.py:170
  101.7 1.8 collective-permute-start.21
  103.9 7.5 %collective-permute-done.20 = bf16[32,4096]{1,0:T(8,128)(2,1)S(1)} collective-permute-done((bf16[32,4096]{1,0:T(8,128)(2,1)S(1)}, bf16[32,4096]{1,0:T(8,128)(2,1)S(1)}, u32[]{:S(2)}, u32[]{:S(2)}) %collective-permute-start.20) | collective-permute-done | bytes 262176 | tf_op jit(solution)/shard_map/ppermute | solution.py:172
  111.6 1.3 copy-done.9
  113.0 5.3 %multiply_convert_fusion.2.refs_0_ = bf16[512,2048]{1,0:T(8,128)(2,1)} fusion(f32[512,2048]{1,0:T(8,128)S(1)} %copy-done.6, bf16[512,2048]{1,0:T(8,128)(2,1)S(1)} %collective-permute-done.11, f32[512,2048]{1,0:T(8,128)S(1)} %copy-done.5, bf16[512,2048]{1,0:T(8,128)(2,1)} %collective-permute-done.8), kind=kLoop, calls=%fused_computation.3 | loop fusion | flops 10485760 | bytes 14680064 | tf_op jit(solution)/shard_map/convert_element_type | solution.py:230
  118.3 9.6 %shard_map.121.refs_3_ = f32[512,2048]{1,0:T(8,128)} custom-call(bf16[512,2048]{1,0:T(8,128)(2,1)} %multiply_convert_fusion.2.refs_0_, bf16[2048,4096]{1,0:T(8,128)(2,1)} %refs_1_.11, s32[16,32]{1,0:T(8,128)S(1)} %copy-done, bf16[64,4096]{1,0:T(8,128)(2,1)S(1)} %collective-permute-done.12.refs_3_, bf16[64,4096]{1,0:T(8,128)(2,1)S(1)} %collective-permute-done.13.refs_4_), custom_call_target="tpu_custom_call" | custom-call | flops 4294967296 | bytes 23070720 | tf_op jit(solution)/shard_map/pallas_call | solution.py:44
  127.9 2.0 fusion.22
  129.9 9.8 %shard_map.122 = f32[512,2048]{1,0:T(8,128)} custom-call(bf16[512,2048]{1,0:T(8,128)(2,1)} %multiply_convert_fusion.2.refs_0_, bf16[2048,4096]{1,0:T(8,128)(2,1)} %refs_1_.11, s32[16,32]{1,0:T(8,128)S(1)} %copy-done, f32[512,2048]{1,0:T(8,128)} %shard_map.121.refs_3_, bf16[64,4096]{1,0:T(8,128)(2,1)S(1)} %collective-permute-done.14.refs_4_, ...), custom_call_target="tpu_custom_call" | custom-call | flops 4294967296 | bytes 23070720 | tf_op jit(solution)/shard_map/pallas_call | solution.py:44
  139.6 1.3 fusion.23
  141.0 2.1 collective-permute-start.18
  143.1 10.0 %shard_map.123 = f32[512,1024]{1,0:T(8,128)} custom-call(bf16[512,4096]{1,0:T(8,128)(2,1)} %copy-done.1, bf16[2048,4096]{1,0:T(8,128)(2,1)} %refs_1_.11, s32[16,32]{1,0:T(8,128)S(1)} %copy-done, bf16[64,2048]{1,0:T(8,128)(2,1)S(1)} %get-tuple-element.23.refs_3_, bf16[64,2048]{1,0:T(8,128)(2,1)S(1)} %get-tuple-element.24.refs_4_), custom_call_target="tpu_custom_call" | custom-call | flops 4294967296 | bytes 23070720 | tf_op jit(solution)/shard_map/pallas_call | solution.py:44
  153.1 2.4 fusion.21
  155.6 2.2 collective-permute-start.19
  157.8 2.3 fusion.20
  160.2 10.0 %shard_map.124 = f32[512,1024]{1,0:T(8,128)} custom-call(bf16[512,4096]{1,0:T(8,128)(2,1)} %copy-done.1, bf16[2048,4096]{1,0:T(8,128)(2,1)} %refs_1_.11, s32[16,32]{1,0:T(8,128)S(1)} %copy-done, bf16[64,4096]{1,0:T(8,128)(2,1)S(1)} %pad_maximum_fusion.1.refs_3_, bf16[64,4096]{1,0:T(8,128)(2,1)S(1)} %pad_maximum_fusion.2.refs_4_), custom_call_target="tpu_custom_call" | custom-call | flops 4294967296 | bytes 23070720 | tf_op jit(solution)/shard_map/pallas_call | solution.py:44
  170.3 1.6 fusion.5
  171.9 12.6 %collective-permute-done.17 = bf16[64,4096]{1,0:T(8,128)(2,1)S(1)} collective-permute-done((bf16[64,4096]{1,0:T(8,128)(2,1)S(1)}, bf16[64,4096]{1,0:T(8,128)(2,1)S(1)}, u32[]{:S(2)}, u32[]{:S(2)}) %collective-permute-start.17) | collective-permute-done | bytes 524320 | tf_op jit(solution)/shard_map/ppermute | solution.py:197
  184.5 1.3 fusion.4
  185.9 0.4 add.73
  186.3 0.4 add.74
  186.7 1.8 copy-done.7
  188.5 0.6 copy-done.10
  189.1 5.0 %multiply_convert_fusion = (bf16[512,2048]{1,0:T(8,128)(2,1)}, bf16[512,2048]{1,0:T(8,128)(2,1)}) fusion(f32[512,1024]{1,0:T(8,128)S(1)} %add.74, f32[512,1024]{1,0:T(8,128)S(1)} %add.73, f32[512,2048]{1,0:T(8,128)S(1)} %copy-done.5, bf16[512,2048]{1,0:T(8,128)(2,1)} %collective-permute-done.8, f32[512,2048]{1,0:T(8,128)S(1)} %copy-done.7, ...), kind=kLoop, calls=%fused_computation.1 | loop fusion | flops 18874368 | bytes 20971520 | tf_op jit(solution)/shard_map/convert_element_type | solution.py:247
  194.4 1.7 collective-permute-start.26
  196.1 15.9 %shard_map.125.refs_6_.refs_3_ = f32[512,2048]{1,0:T(8,128)} custom-call(bf16[512,2048]{1,0:T(8,128)(2,1)} %get-tuple-element.30.refs_0_.refs_1_, bf16[512,2048]{1,0:T(8,128)(2,1)} %get-tuple-element.29.refs_1_, bf16[4096,2048]{1,0:T(8,128)(2,1)} %refs_2_.17, bf16[4096,2048]{1,0:T(8,128)(2,1)} %refs_3_.3, s32[32,16]{1,0:T(8,128)S(1)} %copy.14.refs_2_.refs_4_, ...), custom_call_target="tpu_custom_call" | custom-call | flops 8589934592 | bytes 41947136 | tf_op jit(solution)/shard_map/pallas_call | solution.py:44
  212.0 1.3 fusion.19
  213.8 1.8 collective-permute-start.27
  215.6 15.7 %shard_map.126.refs_4_ = f32[512,2048]{1,0:T(8,128)} custom-call(bf16[512,2048]{1,0:T(8,128)(2,1)} %get-tuple-element.30.refs_0_.refs_1_, bf16[512,2048]{1,0:T(8,128)(2,1)} %get-tuple-element.29.refs_1_, bf16[4096,2048]{1,0:T(8,128)(2,1)} %refs_2_.17, bf16[4096,2048]{1,0:T(8,128)(2,1)} %refs_3_.3, s32[32,16]{1,0:T(8,128)S(1)} %copy.14.refs_2_.refs_4_, ...), custom_call_target="tpu_custom_call" | custom-call | flops 8589934592 | bytes 41947136 | tf_op jit(solution)/shard_map/pallas_call | solution.py:44
  231.4 1.3 fusion.17
  233.0 1.7 collective-permute-start.32
  234.7 9.2 %shard_map.129.refs_5_ = bf16[2048,4096]{1,0:T(8,128)(2,1)} custom-call(bf16[512,2048]{1,0:T(8,128)(2,1)} %multiply_convert_fusion.2.refs_0_, bf16[512,4096]{1,0:T(8,128)(2,1)} %copy-done.1, s32[16,32]{1,0:T(8,128)S(1)} %copy-done, f32[512,2048]{1,0:T(8,128)} %shard_map.125.refs_6_.refs_3_, f32[512,2048]{1,0:T(8,128)} %shard_map.126.refs_4_, ...), custom_call_target="tpu_custom_call" | custom-call | flops 4294967296 | bytes 23070720 | tf_op jit(solution)/shard_map/pallas_call | solution.py:44
  243.9 0.4 fusion.18
  244.3 1.8 collective-permute-start.33
  246.1 1.2 fusion.14
  247.4 0.6 collective-permute-start.29
  247.9 14.1 %shard_map.127 = bf16[4096,2048]{1,0:T(8,128)(2,1)} custom-call(bf16[512,4096]{1,0:T(8,128)(2,1)} %copy-done.19, bf16[512,2048]{1,0:T(8,128)(2,1)} %get-tuple-element.30.refs_0_.refs_1_, s32[32,16]{1,0:T(8,128)S(1)} %copy.14.refs_2_.refs_4_, bf16[64,4096]{1,0:T(8,128)(2,1)S(1)} %pad_maximum_fusion.3.refs_3_, bf16[64,4096]{1,0:T(8,128)(2,1)S(1)} %pad_maximum_fusion.4.refs_4_), custom_call_target="tpu_custom_call" | custom-call | flops 8589934592 | bytes 23070720 | tf_op jit(solution)/shard_map/pallas_call | solution.py:44
  262.1 2.0 fusion.2
  264.6 1.8 collective-permute-start.34
  266.4 9.8 %collective-permute-done.30 = bf16[64,4096]{1,0:T(8,128)(2,1)S(1)} collective-permute-done((bf16[64,4096]{1,0:T(8,128)(2,1)S(1)}, bf16[64,4096]{1,0:T(8,128)(2,1)S(1)}, u32[]{:S(2)}, u32[]{:S(2)}) %collective-permute-start.30) | collective-permute-done | bytes 524320 | tf_op jit(solution)/shard_map/ppermute | solution.py:197
  276.7 1.8 collective-permute-start.35
  278.5 14.1 %shard_map.128 = bf16[4096,2048]{1,0:T(8,128)(2,1)} custom-call(bf16[512,4096]{1,0:T(8,128)(2,1)} %copy-done.19, bf16[512,2048]{1,0:T(8,128)(2,1)} %get-tuple-element.29.refs_1_, s32[32,16]{1,0:T(8,128)S(1)} %copy.15.refs_2_.refs_5_, bf16[64,4096]{1,0:T(8,128)(2,1)S(1)} %fusion.10.refs_3_, bf16[64,4096]{1,0:T(8,128)(2,1)S(1)} %fusion.12.refs_4_), custom_call_target="tpu_custom_call" | custom-call | flops 8589934592 | bytes 23070720 | tf_op jit(solution)/shard_map/pallas_call | solution.py:44
  292.7 9.2 %shard_map.130 = bf16[2048,4096]{1,0:T(8,128)(2,1)} custom-call(bf16[512,2048]{1,0:T(8,128)(2,1)} %multiply_convert_fusion.2.refs_0_, bf16[512,4096]{1,0:T(8,128)(2,1)} %copy-done.1, s32[16,32]{1,0:T(8,128)S(1)} %copy-done, bf16[64,4096]{1,0:T(8,128)(2,1)S(1)} %fusion.9.refs_3_, ...), custom_call_target="tpu_custom_call", output_to_operand_aliasing={{}: (5, {})} | custom-call | flops 4294967296 | bytes 23070720 | tf_op jit(solution)/shard_map/pallas_call | solution.py:44
  301.9 1.0 fusion.8
  (110 shorter events, 4.0 us)
Async XLA Ops:
  0.6 15.2 %collective-permute-start = (bf16[64,4096]{1,0:T(8,128)(2,1)}, bf16[64,4096]{1,0:T(8,128)(2,1)S(1)}, u32[]{:S(2)}, u32[]{:S(2)}) collective-permute-start(bf16[64,4096]{1,0:T(8,128)(2,1)} %param.8), channel_id=1, source_target_pairs={{2,0},{4,2},{6,4},{7,6},{5,7},{3,5},{1,3},{0,1},{10,8},{12,10},{14... | collective-permute-start | bytes 1572872 | tf_op jit(solution)/shard_map/ppermute | solution.py:170
  3.6 13.9 %collective-permute-start.3 = (bf16[64,4096]{1,0:T(8,128)(2,1)}, bf16[64,4096]{1,0:T(8,128)(2,1)S(1)}, u32[]{:S(2)}, u32[]{:S(2)}) collective-permute-start(bf16[64,4096]{1,0:T(8,128)(2,1)} %param.8), channel_id=1, source_target_pairs={{0,2},{2,4},{4,6},{6,7},{7,5},{5,3},{3,1},{1,0},{8,10},{10,12},{12... | collective-permute-start | bytes 1572872 | tf_op jit(solution)/shard_map/ppermute | solution.py:169
  15.8 13.1 %collective-permute-start.1 = (bf16[64,4096]{1,0:T(8,128)(2,1)S(1)}, bf16[64,4096]{1,0:T(8,128)(2,1)S(1)}, u32[]{:S(2)}, u32[]{:S(2)}) collective-permute-start(bf16[64,4096]{1,0:T(8,128)(2,1)S(1)} %collective-permute-done), channel_id=1, source_target_pairs={{2,0},{4,2},{6,4},{7,6},{5,7},{3,5},{1,3},{0,1},{10,8},{12,10},{14... | collective-permute-start | bytes 1572872 | tf_op jit(solution)/shard_map/ppermute | solution.py:170
  17.5 12.8 %collective-permute-start.4 = (bf16[64,4096]{1,0:T(8,128)(2,1)S(1)}, bf16[64,4096]{1,0:T(8,128)(2,1)S(1)}, u32[]{:S(2)}, u32[]{:S(2)}) collective-permute-start(bf16[64,4096]{1,0:T(8,128)(2,1)S(1)} %collective-permute-done.3), channel_id=1, source_target_pairs={{0,2},{2,4},{4,6},{6,7},{7,5},{5,3},{3,1},{1,0},{8,10},{10,12},{12... | collective-permute-start | bytes 1572872 | tf_op jit(solution)/shard_map/ppermute | solution.py:169
  20.5 28.5 %copy-start.18 = (bf16[64,4096]{1,0:T(8,128)(2,1)S(1)}, bf16[64,4096]{1,0:T(8,128)(2,1)}, u32[]{:S(2)}) copy-start(bf16[64,4096]{1,0:T(8,128)(2,1)} %param.9) | copy-start | bytes 1572868
  29.0 12.2 %collective-permute-start.2 = (bf16[64,4096]{1,0:T(8,128)(2,1)S(1)}, bf16[64,4096]{1,0:T(8,128)(2,1)S(1)}, u32[]{:S(2)}, u32[]{:S(2)}) collective-permute-start(bf16[64,4096]{1,0:T(8,128)(2,1)S(1)} %collective-permute-done.1), channel_id=1, source_target_pairs={{2,0},{4,2},{6,4},{7,6},{5,7},{3,5},{1,3},{0,1},{10,8},{12,10},{14... | collective-permute-start | bytes 1572872 | tf_op jit(solution)/shard_map/ppermute | solution.py:170
  30.3 12.1 %collective-permute-start.5 = (bf16[64,4096]{1,0:T(8,128)(2,1)S(1)}, bf16[64,4096]{1,0:T(8,128)(2,1)S(1)}, u32[]{:S(2)}, u32[]{:S(2)}) collective-permute-start(bf16[64,4096]{1,0:T(8,128)(2,1)S(1)} %collective-permute-done.4), channel_id=1, source_target_pairs={{0,2},{2,4},{4,6},{6,7},{7,5},{5,3},{3,1},{1,0},{8,10},{10,12},{12... | collective-permute-start | bytes 1572872 | tf_op jit(solution)/shard_map/ppermute | solution.py:169
  41.2 7.7 %collective-permute-start.7 = (bf16[32,4096]{1,0:T(8,128)(2,1)S(1)}, bf16[32,4096]{1,0:T(8,128)(2,1)S(1)}, u32[]{:S(2)}, u32[]{:S(2)}) collective-permute-start(bf16[32,4096]{1,0:T(8,128)(2,1)S(1)} %slice.149), channel_id=1, source_target_pairs={{2,0},{4,2},{6,4},{7,6},{5,7},{3,5},{1,3},{0,1},{10,8},{12,10},{14... | collective-permute-start | bytes 786440 | tf_op jit(solution)/shard_map/ppermute | solution.py:173
  42.4 6.4 %collective-permute-start.6 = (bf16[32,4096]{1,0:T(8,128)(2,1)S(1)}, bf16[32,4096]{1,0:T(8,128)(2,1)S(1)}, u32[]{:S(2)}, u32[]{:S(2)}) collective-permute-start(bf16[32,4096]{1,0:T(8,128)(2,1)S(1)} %slice.148), channel_id=1, source_target_pairs={{0,2},{2,4},{4,6},{6,7},{7,5},{5,3},{3,1},{1,0},{8,10},{10,12},{12... | collective-permute-start | bytes 786440 | tf_op jit(solution)/shard_map/ppermute | solution.py:172
  49.0 2.1 copy-start.19
  49.0 19.1 %collective-permute-start.10 = (bf16[64,4096]{1,0:T(8,128)(2,1)S(1)}, bf16[64,4096]{1,0:T(8,128)(2,1)S(1)}, u32[]{:S(2)}, u32[]{:S(2)}) collective-permute-start(bf16[64,4096]{1,0:T(8,128)(2,1)S(1)} %copy-done.18), channel_id=1, source_target_pairs={{2,0},{4,2},{6,4},{7,6},{5,7},{3,5},{1,3},{0,1},{10,8},{12,10},{14... | collective-permute-start | bytes 1572872 | tf_op jit(solution)/shard_map/ppermute | solution.py:170
  50.7 19.1 %collective-permute-start.9 = (bf16[64,4096]{1,0:T(8,128)(2,1)S(1)}, bf16[64,4096]{1,0:T(8,128)(2,1)S(1)}, u32[]{:S(2)}, u32[]{:S(2)}) collective-permute-start(bf16[64,4096]{1,0:T(8,128)(2,1)S(1)} %copy-done.18), channel_id=1, source_target_pairs={{0,2},{2,4},{4,6},{6,7},{7,5},{5,3},{3,1},{1,0},{8,10},{10,12},{12... | collective-permute-start | bytes 1572872 | tf_op jit(solution)/shard_map/ppermute | solution.py:169
  68.1 43.5 %collective-permute-start.8 = (bf16[512,2048]{1,0:T(8,128)(2,1)}, bf16[512,2048]{1,0:T(8,128)(2,1)}, u32[]{:S(2)}, u32[]{:S(2)}) collective-permute-start(bf16[512,2048]{1,0:T(8,128)(2,1)} %get-tuple-element.19.refs_3_), channel_id=1, source_target_pairs={{0,8},{8,0},{1,9},{9,1},{2,10},{10,2},{3,11},{11,3},{4,12},{12,4},... | collective-permute-start | bytes 6291464 | tf_op jit(solution)/shard_map/ppermute | solution.py:218
  68.2 19.2 %collective-permute-start.13 = (bf16[64,4096]{1,0:T(8,128)(2,1)S(1)}, bf16[64,4096]{1,0:T(8,128)(2,1)S(1)}, u32[]{:S(2)}, u32[]{:S(2)}) collective-permute-start(bf16[64,4096]{1,0:T(8,128)(2,1)S(1)} %collective-permute-done.10.refs_5_), channel_id=1, source_target_pairs={{2,0},{4,2},{6,4},{7,6},{5,7},{3,5},{1,3},{0,1},{10,8},{12,10},{14... | collective-permute-start | bytes 1572872 | tf_op jit(solution)/shard_map/ppermute | solution.py:170
  69.8 19.5 %collective-permute-start.12 = (bf16[64,4096]{1,0:T(8,128)(2,1)S(1)}, bf16[64,4096]{1,0:T(8,128)(2,1)S(1)}, u32[]{:S(2)}, u32[]{:S(2)}) collective-permute-start(bf16[64,4096]{1,0:T(8,128)(2,1)S(1)} %collective-permute-done.9.refs_4_), channel_id=1, source_target_pairs={{0,2},{2,4},{4,6},{6,7},{7,5},{5,3},{3,1},{1,0},{8,10},{10,12},{12... | collective-permute-start | bytes 1572872 | tf_op jit(solution)/shard_map/ppermute | solution.py:169
  87.3 25.7 %copy-start.5 = (f32[512,2048]{1,0:T(8,128)S(1)}, f32[512,2048]{1,0:T(8,128)}, u32[]{:S(2)}) copy-start(f32[512,2048]{1,0:T(8,128)} %get-tuple-element.18) | copy-start | bytes 12582916
  87.3 25.7 %copy-start.6 = (f32[512,2048]{1,0:T(8,128)S(1)}, f32[512,2048]{1,0:T(8,128)}, u32[]{:S(2)}) copy-start(f32[512,2048]{1,0:T(8,128)} %get-tuple-element.21) | copy-start | bytes 12582916
  87.3 24.4 %collective-permute-start.11 = (bf16[512,2048]{1,0:T(8,128)(2,1)}, bf16[512,2048]{1,0:T(8,128)(2,1)S(1)}, u32[]{:S(2)}, u32[]{:S(2)}) collective-permute-start(bf16[512,2048]{1,0:T(8,128)(2,1)} %get-tuple-element.22), channel_id=1, source_target_pairs={{0,8},{8,0},{1,9},{9,1},{2,10},{10,2},{3,11},{11,3},{4,12},{12,4},... | collective-permute-start | bytes 6291464 | tf_op jit(solution)/shard_map/ppermute | solution.py:218
  87.3 14.3 %collective-permute-start.15 = (bf16[64,4096]{1,0:T(8,128)(2,1)S(1)}, bf16[64,4096]{1,0:T(8,128)(2,1)S(1)}, u32[]{:S(2)}, u32[]{:S(2)}) collective-permute-start(bf16[64,4096]{1,0:T(8,128)(2,1)S(1)} %collective-permute-done.13.refs_4_), channel_id=1, source_target_pairs={{2,0},{4,2},{6,4},{7,6},{5,7},{3,5},{1,3},{0,1},{10,8},{12,10},{14... | collective-permute-start | bytes 1572872 | tf_op jit(solution)/shard_map/ppermute | solution.py:170
  89.3 14.2 %collective-permute-start.14 = (bf16[64,4096]{1,0:T(8,128)(2,1)S(1)}, bf16[64,4096]{1,0:T(8,128)(2,1)S(1)}, u32[]{:S(2)}, u32[]{:S(2)}) collective-permute-start(bf16[64,4096]{1,0:T(8,128)(2,1)S(1)} %collective-permute-done.12.refs_3_), channel_id=1, source_target_pairs={{0,2},{2,4},{4,6},{6,7},{7,5},{5,3},{3,1},{1,0},{8,10},{10,12},{12... | collective-permute-start | bytes 1572872 | tf_op jit(solution)/shard_map/ppermute | solution.py:169
  101.7 9.7 %collective-permute-start.21 = (bf16[32,4096]{1,0:T(8,128)(2,1)S(1)}, bf16[32,4096]{1,0:T(8,128)(2,1)S(1)}, u32[]{:S(2)}, u32[]{:S(2)}) collective-permute-start(bf16[32,4096]{1,0:T(8,128)(2,1)S(1)} %slice.165), channel_id=1, source_target_pairs={{2,0},{4,2},{6,4},{7,6},{5,7},{3,5},{1,3},{0,1},{10,8},{12,10},{14... | collective-permute-start | bytes 786440 | tf_op jit(solution)/shard_map/ppermute | solution.py:173
  103.5 7.9 %collective-permute-start.20 = (bf16[32,4096]{1,0:T(8,128)(2,1)S(1)}, bf16[32,4096]{1,0:T(8,128)(2,1)S(1)}, u32[]{:S(2)}, u32[]{:S(2)}) collective-permute-start(bf16[32,4096]{1,0:T(8,128)(2,1)S(1)} %slice.164), channel_id=1, source_target_pairs={{0,2},{2,4},{4,6},{6,7},{7,5},{5,3},{3,1},{1,0},{8,10},{10,12},{12... | collective-permute-start | bytes 786440 | tf_op jit(solution)/shard_map/ppermute | solution.py:172
  111.6 6.7 %copy-start.1 = (bf16[512,4096]{1,0:T(8,128)(2,1)}, bf16[512,4096]{1,0:T(8,128)(2,1)S(1)}, u32[]{:S(2)}) copy-start(bf16[512,4096]{1,0:T(8,128)(2,1)S(1)} %constant_dynamic-update-slice_fusion.9.refs_0_.refs_1_) | copy-start | bytes 12582916
  111.6 1.4 copy-start.9
  113.0 5.3 %copy-start = (s32[16,32]{1,0:T(8,128)S(1)}, s32[16,32]{1,0:T(8,128)}, u32[]{:S(2)}) copy-start(s32[16,32]{1,0:T(8,128)} %refs_2_.19) | copy-start | bytes 6148
  140.9 12.2 %copy-start.8 = (f32[512,2048]{1,0:T(8,128)S(1)}, f32[512,2048]{1,0:T(8,128)}, u32[]{:S(2)}) copy-start(f32[512,2048]{1,0:T(8,128)} %shard_map.122) | copy-start | bytes 12582916
  140.9 16.8 %collective-permute-start.16 = (bf16[64,2048]{1,0:T(8,128)(2,1)S(1)}, bf16[64,2048]{1,0:T(8,128)(2,1)}, u32[]{:S(2)}, u32[]{:S(2)}) collective-permute-start(bf16[64,2048]{1,0:T(8,128)(2,1)S(1)} %get-tuple-element.23.refs_3_), channel_id=1, source_target_pairs={{0,2},{2,4},{4,6},{6,7},{7,5},{5,3},{3,1},{1,0},{8,10},{10,12},{12... | collective-permute-start | bytes 786440 | tf_op jit(solution)/shard_map/ppermute | solution.py:191
  141.0 12.1 %collective-permute-start.18 = (bf16[64,2048]{1,0:T(8,128)(2,1)S(1)}, bf16[64,2048]{1,0:T(8,128)(2,1)}, u32[]{:S(2)}, u32[]{:S(2)}) collective-permute-start(bf16[64,2048]{1,0:T(8,128)(2,1)S(1)} %get-tuple-element.24.refs_4_), channel_id=1, source_target_pairs={{2,0},{4,2},{6,4},{7,6},{5,7},{3,5},{1,3},{0,1},{10,8},{12,10},{14... | collective-permute-start | bytes 786440 | tf_op jit(solution)/shard_map/ppermute | solution.py:191
  153.1 2.4 copy-start.17
  153.1 4.7 %copy-start.4 = (f32[512,2048]{1,0:T(8,128)S(1)}, f32[512,2048]{1,0:T(8,128)}, u32[]{:S(2)}) copy-start(f32[512,2048]{1,0:T(8,128)} %shard_map.121.refs_3_) | copy-start | bytes 12582916
  153.1 32.7 %collective-permute-start.22 = (f32[512,1024]{1,0:T(8,128)}, f32[512,1024]{1,0:T(8,128)S(1)}, u32[]{:S(2)}, u32[]{:S(2)}) collective-permute-start(f32[512,1024]{1,0:T(8,128)} %shard_map.123), channel_id=1, source_target_pairs={{0,8},{8,0},{1,9},{9,1},{2,10},{10,2},{3,11},{11,3},{4,12},{12,4},... | collective-permute-start | bytes 6291464 | tf_op jit(solution)/shard_map/ppermute | solution.py:218
  155.6 14.8 %collective-permute-start.19 = (bf16[64,4096]{1,0:T(8,128)(2,1)S(1)}, bf16[64,4096]{1,0:T(8,128)(2,1)}, u32[]{:S(2)}, u32[]{:S(2)}) collective-permute-start(bf16[64,4096]{1,0:T(8,128)(2,1)S(1)} %pad_maximum_fusion.2.refs_4_), channel_id=1, source_target_pairs={{2,0},{4,2},{6,4},{7,6},{5,7},{3,5},{1,3},{0,1},{10,8},{12,10},{14... | collective-permute-start | bytes 1572872 | tf_op jit(solution)/shard_map/ppermute | solution.py:198
  160.2 24.4 %copy-start.16 = (f32[64,2048]{1,0:T(8,128)S(1)}, f32[64,2048]{1,0:T(8,128)}, u32[]{:S(2)}) copy-start(f32[64,2048]{1,0:T(8,128)} %get-tuple-element.57) | copy-start | bytes 1572868
  170.2 15.7 %copy-start.11 = (f32[512,1024]{1,0:T(8,128)S(1)}, f32[512,1024]{1,0:T(8,128)}, u32[]{:S(2)}) copy-start(f32[512,1024]{1,0:T(8,128)} %shard_map.123) | copy-start | bytes 6291460
  170.2 16.1 %collective-permute-start.23 = (f32[512,1024]{1,0:T(8,128)}, f32[512,1024]{1,0:T(8,128)S(1)}, u32[]{:S(2)}, u32[]{:S(2)}) collective-permute-start(f32[512,1024]{1,0:T(8,128)} %shard_map.124), channel_id=1, source_target_pairs={{0,8},{8,0},{1,9},{9,1},{2,10},{10,2},{3,11},{11,3},{4,12},{12,4},... | collective-permute-start | bytes 6291464 | tf_op jit(solution)/shard_map/ppermute | solution.py:218
  170.3 14.3 %collective-permute-start.17 = (bf16[64,4096]{1,0:T(8,128)(2,1)S(1)}, bf16[64,4096]{1,0:T(8,128)(2,1)S(1)}, u32[]{:S(2)}, u32[]{:S(2)}) collective-permute-start(bf16[64,4096]{1,0:T(8,128)(2,1)S(1)} %pad_maximum_fusion.1.refs_3_), channel_id=1, source_target_pairs={{0,2},{2,4},{4,6},{6,7},{7,5},{5,3},{3,1},{1,0},{8,10},{10,12},{12... | collective-permute-start | bytes 1572872 | tf_op jit(solution)/shard_map/ppermute | solution.py:197
  184.5 1.8 copy-start.12
  186.3 2.2 copy-start.7
  186.3 2.8 copy-start.10
  194.1 19.2 %collective-permute-start.24 = (bf16[64,4096]{1,0:T(8,128)(2,1)S(1)}, bf16[64,4096]{1,0:T(8,128)(2,1)S(1)}, u32[]{:S(2)}, u32[]{:S(2)}) collective-permute-start(bf16[64,4096]{1,0:T(8,128)(2,1)S(1)} %fusion.4), channel_id=1, source_target_pairs={{0,2},{2,4},{4,6},{6,7},{7,5},{5,3},{3,1},{1,0},{8,10},{10,12},{12... | collective-permute-start | bytes 1572872 | tf_op jit(solution)/shard_map/ppermute | solution.py:197
  194.4 19.3 %collective-permute-start.26 = (bf16[64,4096]{1,0:T(8,128)(2,1)S(1)}, bf16[64,4096]{1,0:T(8,128)(2,1)S(1)}, u32[]{:S(2)}, u32[]{:S(2)}) collective-permute-start(bf16[64,4096]{1,0:T(8,128)(2,1)S(1)} %fusion.5), channel_id=1, source_target_pairs={{2,0},{4,2},{6,4},{7,6},{5,7},{3,5},{1,3},{0,1},{10,8},{12,10},{14... | collective-permute-start | bytes 1572872 | tf_op jit(solution)/shard_map/ppermute | solution.py:198
  196.1 17.1 %copy-start.13 = (f32[64,2048]{1,0:T(8,128)S(1)}, f32[64,2048]{1,0:T(8,128)}, u32[]{:S(2)}) copy-start(f32[64,2048]{1,0:T(8,128)} %get-tuple-element.53) | copy-start | bytes 1572868
  196.1 17.2 %copy-start.15 = (f32[64,2048]{1,0:T(8,128)S(1)}, f32[64,2048]{1,0:T(8,128)}, u32[]{:S(2)}) copy-start(f32[64,2048]{1,0:T(8,128)} %get-tuple-element.47) | copy-start | bytes 1572868
  196.1 17.6 %copy-start.14 = (f32[64,2048]{1,0:T(8,128)S(1)}, f32[64,2048]{1,0:T(8,128)}, u32[]{:S(2)}) copy-start(f32[64,2048]{1,0:T(8,128)} %get-tuple-element.48) | copy-start | bytes 1572868
  213.4 48.7 %collective-permute-start.25 = (bf16[64,4096]{1,0:T(8,128)(2,1)S(1)}, bf16[64,4096]{1,0:T(8,128)(2,1)}, u32[]{:S(2)}, u32[]{:S(2)}) collective-permute-start(bf16[64,4096]{1,0:T(8,128)(2,1)S(1)} %fusion.3.refs_7_), channel_id=1, source_target_pairs={{0,2},{2,4},{4,6},{6,7},{7,5},{5,3},{3,1},{1,0},{8,10},{10,12},{12... | collective-permute-start | bytes 1572872 | tf_op jit(solution)/shard_map/ppermute | solution.py:202
  213.8 48.3 %collective-permute-start.27 = (bf16[64,4096]{1,0:T(8,128)(2,1)S(1)}, bf16[64,4096]{1,0:T(8,128)(2,1)S(1)}, u32[]{:S(2)}, u32[]{:S(2)}) collective-permute-start(bf16[64,4096]{1,0:T(8,128)(2,1)S(1)} %fusion.6.refs_8_), channel_id=1, source_target_pairs={{2,0},{4,2},{6,4},{7,6},{5,7},{3,5},{1,3},{0,1},{10,8},{12,10},{14... | collective-permute-start | bytes 1572872 | tf_op jit(solution)/shard_map/ppermute | solution.py:203
  232.6 11.3 %copy-start.3 = (f32[512,2048]{1,0:T(8,128)S(1)}, f32[512,2048]{1,0:T(8,128)}, u32[]{:S(2)}) copy-start(f32[512,2048]{1,0:T(8,128)} %shard_map.126.refs_4_) | copy-start | bytes 12582916
  232.6 13.5 %collective-permute-start.28 = (bf16[64,2048]{1,0:T(8,128)(2,1)S(1)}, bf16[64,2048]{1,0:T(8,128)(2,1)}, u32[]{:S(2)}, u32[]{:S(2)}) collective-permute-start(bf16[64,2048]{1,0:T(8,128)(2,1)S(1)} %get-tuple-element.27.refs_5_), channel_id=1, source_target_pairs={{0,2},{2,4},{4,6},{6,7},{7,5},{5,3},{3,1},{1,0},{8,10},{10,12},{12... | collective-permute-start | bytes 786440 | tf_op jit(solution)/shard_map/ppermute | solution.py:191
  233.0 10.9 %collective-permute-start.32 = (bf16[64,2048]{1,0:T(8,128)(2,1)S(1)}, bf16[64,2048]{1,0:T(8,128)(2,1)S(1)}, u32[]{:S(2)}, u32[]{:S(2)}) collective-permute-start(bf16[64,2048]{1,0:T(8,128)(2,1)S(1)} %get-tuple-element.28.refs_6_), channel_id=1, source_target_pairs={{2,0},{4,2},{6,4},{7,6},{5,7},{3,5},{1,3},{0,1},{10,8},{12,10},{14... | collective-permute-start | bytes 786440 | tf_op jit(solution)/shard_map/ppermute | solution.py:191
  243.9 2.2 copy-start.2
  244.3 20.2 %collective-permute-start.33 = (bf16[64,4096]{1,0:T(8,128)(2,1)S(1)}, bf16[64,4096]{1,0:T(8,128)(2,1)S(1)}, u32[]{:S(2)}, u32[]{:S(2)}) collective-permute-start(bf16[64,4096]{1,0:T(8,128)(2,1)S(1)} %pad_maximum_fusion.4.refs_4_), channel_id=1, source_target_pairs={{2,0},{4,2},{6,4},{7,6},{5,7},{3,5},{1,3},{0,1},{10,8},{12,10},{14... | collective-permute-start | bytes 1572872 | tf_op jit(solution)/shard_map/ppermute | solution.py:198
  247.4 16.7 %collective-permute-start.29 = (bf16[64,4096]{1,0:T(8,128)(2,1)S(1)}, bf16[64,4096]{1,0:T(8,128)(2,1)S(1)}, u32[]{:S(2)}, u32[]{:S(2)}) collective-permute-start(bf16[64,4096]{1,0:T(8,128)(2,1)S(1)} %pad_maximum_fusion.3.refs_3_), channel_id=1, source_target_pairs={{0,2},{2,4},{4,6},{6,7},{7,5},{5,3},{3,1},{1,0},{8,10},{10,12},{12... | collective-permute-start | bytes 1572872 | tf_op jit(solution)/shard_map/ppermute | solution.py:197
  264.2 12.0 %collective-permute-start.30 = (bf16[64,4096]{1,0:T(8,128)(2,1)S(1)}, bf16[64,4096]{1,0:T(8,128)(2,1)S(1)}, u32[]{:S(2)}, u32[]{:S(2)}) collective-permute-start(bf16[64,4096]{1,0:T(8,128)(2,1)S(1)} %fusion.10.refs_3_), channel_id=1, source_target_pairs={{0,2},{2,4},{4,6},{6,7},{7,5},{5,3},{3,1},{1,0},{8,10},{10,12},{12... | collective-permute-start | bytes 1572872 | tf_op jit(solution)/shard_map/ppermute | solution.py:197
  264.6 12.0 %collective-permute-start.34 = (bf16[64,4096]{1,0:T(8,128)(2,1)S(1)}, bf16[64,4096]{1,0:T(8,128)(2,1)S(1)}, u32[]{:S(2)}, u32[]{:S(2)}) collective-permute-start(bf16[64,4096]{1,0:T(8,128)(2,1)S(1)} %fusion.12.refs_4_), channel_id=1, source_target_pairs={{2,0},{4,2},{6,4},{7,6},{5,7},{3,5},{1,3},{0,1},{10,8},{12,10},{14... | collective-permute-start | bytes 1572872 | tf_op jit(solution)/shard_map/ppermute | solution.py:198
  276.3 25.6 %collective-permute-start.31 = (bf16[64,4096]{1,0:T(8,128)(2,1)S(1)}, bf16[64,4096]{1,0:T(8,128)(2,1)S(1)}, u32[]{:S(2)}, u32[]{:S(2)}) collective-permute-start(bf16[64,4096]{1,0:T(8,128)(2,1)S(1)} %fusion.9.refs_3_), channel_id=1, source_target_pairs={{0,2},{2,4},{4,6},{6,7},{7,5},{5,3},{3,1},{1,0},{8,10},{10,12},{12... | collective-permute-start | bytes 1572872 | tf_op jit(solution)/shard_map/ppermute | solution.py:202
  276.7 25.1 %collective-permute-start.35 = (bf16[64,4096]{1,0:T(8,128)(2,1)S(1)}, bf16[64,4096]{1,0:T(8,128)(2,1)S(1)}, u32[]{:S(2)}, u32[]{:S(2)}) collective-permute-start(bf16[64,4096]{1,0:T(8,128)(2,1)S(1)} %fusion.11.refs_4_), channel_id=1, source_target_pairs={{2,0},{4,2},{6,4},{7,6},{5,7},{3,5},{1,3},{0,1},{10,8},{12,10},{14... | collective-permute-start | bytes 1572872 | tf_op jit(solution)/shard_map/ppermute | solution.py:203
